TPU v7x, 32 devices: a whole 2x2x4 slice. The times are simulated.
32 devices in a mesh: grid: 16 (over z, x, core), orb: 2 (over y).
Axes of the slice: x: 2, y: 2, z: 4, core: 2. Of those that a mesh axis runs over, the one named last changes fastest.
Arguments:
- wave: float32 [2, 2, 128, 128, 128], P(None, 'orb', 'grid'), may hold values from -6 to 6
- potential: float32 [128, 128, 128], P('grid'), may hold values from -24 to 24
- occupations: float32 [2], P('orb'), may hold values from 0.01 to 0.1
- centres: int32 [3, 128], replicated, may hold values from 0 to 127, as said below
- species: int32 [128], replicated, may hold values from 0 to 1
- projectors: float32 [2, 16, 8, 256], replicated, may hold values from -0.75 to 0.75
- coupling: float32 [2, 8, 8], replicated, may hold values from -6 to 6
Outputs:
- update: float32 [2, 2, 128, 128, 128], P(None, 'orb', 'grid')
- density: float32 [128, 128, 128], P('grid', 'orb')
Inputs may be any that keep to these rules, and one draw needn't show every extreme that they name: `centres`: each column is a grid point of the cell.
All inputs are finite; a program needn't handle non-finite values.
Results may differ from a plain program's by a relative error of at most 0.0003.
Values sent between devices are 32-bit elements; how exact they have to be, the bound alone decides.
A program may use at most 64 MiB of HBM per device.

v0:
```python
import math

import jax
import jax.numpy as jnp
import numpy as np
from jax import lax
from jax.experimental import pallas as pl
from jax.experimental.pallas import tpu as pltpu
from jax.sharding import PartitionSpec as P

spacing = 0.32
time_step = 0.1
highest = lax.Precision.HIGHEST
VMEM = pl.BlockSpec(memory_space=pltpu.VMEM)
SMEM = pl.BlockSpec(memory_space=pltpu.SMEM)


def params():
    return pltpu.CompilerParams(vmem_limit_bytes=40 * 1024 * 1024)


def second_derivative(extent):
    counts = np.arange(extent)
    signed = np.where(counts < extent // 2, counts, counts - extent)
    waves = signed * (2.0 * math.pi / (extent * spacing))
    angles = (counts[:, None] * counts[None, :] % extent) * (2.0 * math.pi / extent)
    row = np.cos(angles) @ (0.5 * waves**2) / extent
    full = row[(counts[:, None] - counts[None, :]) % extent].astype(np.float32)
    high = full.astype(jnp.bfloat16)
    low = (full - high.astype(np.float32)).astype(jnp.bfloat16)
    return jnp.asarray(high), jnp.asarray(low)


def split(value):
    high = value.astype(jnp.bfloat16)
    low = (value - high.astype(jnp.float32)).astype(jnp.bfloat16)
    return high, low


def mul(left, right):
    def dot(a, b):
        return jnp.dot(a, b, preferred_element_type=jnp.float32)

    return dot(left[0], right[0]) + (dot(left[0], right[1]) + dot(left[1], right[0]))


def pack_kernel(wave_ref, occ_ref, send_ref, density_ref):
    _, orbitals, planes, extent, _ = wave_ref.shape
    count = send_ref.shape[0]
    width = extent // count
    for p in range(planes):
        total = None
        for o in range(orbitals):
            real = wave_ref[0, o, p]
            imag = wave_ref[1, o, p]
            term = occ_ref[o] * (real * real + imag * imag)
            total = term if total is None else total + term
        density_ref[p] = total
        for c in range(2):
            for o in range(orbitals):
                for d in range(count):
                    send_ref[d, c * orbitals + o, pl.ds(p, width, stride=planes), :] = wave_ref[
                        c, o, p, d * width : (d + 1) * width, :
                    ]


def along_x_kernel(held_ref, high_ref, low_ref, out_ref, lined):
    count, rows, both, extent = held_ref.shape
    planes = extent // count
    matrix = (high_ref[...], low_ref[...])
    for r in range(rows):
        for y in range(both // planes):
            block = pl.ds(y * planes, planes)
            if planes % 8 == 0:
                column = held_ref[:, r, block, :].reshape(extent, extent)
            else:
                for s in range(count):
                    lined[s * planes : (s + 1) * planes, :] = held_ref[s, r, block, :]
                column = lined[...]
            result = mul(matrix, split(column))
            if planes % 8 == 0:
                out_ref[:, r, block, :] = result.reshape(count, planes, extent)
            else:
                lined[...] = result
                for s in range(count):
                    out_ref[s, r, block, :] = lined[s * planes : (s + 1) * planes, :]


def list_hits(centres_ref, hits, extent, planes, half_box):
    first_plane = lax.axis_index("grid") * planes

    def look(atom, found):
        start = lax.rem(first_plane - centres_ref[0, atom] + (half_box + extent), extent)
        hits[found] = atom
        meets = jnp.logical_or(start < 2 * half_box, start + planes > extent)
        return found + meets.astype(jnp.int32)

    return lax.fori_loop(0, centres_ref.shape[1], look, jnp.int32(0), unroll=8)


def atom_place(centres_ref, species_ref, atom, extent, planes, box):
    half_box = box // 2
    first_plane = lax.axis_index("grid") * planes
    start_x = lax.rem(first_plane - centres_ref[0, atom] + (half_box + extent), extent)
    start_y = lax.rem(centres_ref[1, atom] + (extent - half_box), extent)
    start_z = lax.rem(centres_ref[2, atom] + (extent - half_box), extent)
    slots = []
    for p in range(planes):
        depth = lax.rem(start_x + p, extent)
        slots.append(species_ref[atom] * (box + 1) + jnp.minimum(depth, box))
    return slots, start_y, start_z


def project_kernel(wave_ref, table_ref, centres_ref, species_ref, coef_ref, padded, sums, hits):
    _, orbitals, planes, extent, _ = wave_ref.shape
    box = table_ref.shape[1]
    lanes = table_ref.shape[2]
    rows = 2 * orbitals
    for c in range(2):
        for o in range(orbitals):
            for p in range(planes):
                at = (c * orbitals + o) * planes + p
                padded[at, :extent, :] = wave_ref[c, o, p]
                padded[at, extent:, :] = wave_ref[c, o, p, :box, :]
    sums[...] = jnp.zeros_like(sums)
    found = list_hits(centres_ref, hits, extent, planes, box // 2)
    lane = lax.broadcasted_iota(jnp.int32, (box, lanes), 1) % box

    def one(step, carry):
        atom = hits[step]
        slots, start_y, start_z = atom_place(
            centres_ref, species_ref, atom, extent, planes, box
        )
        places = lane + start_z
        places = jnp.where(places >= extent, places - extent, places)
        totals = [None] * rows
        for p in range(planes):
            beta = table_ref[slots[p]]
            for r in range(rows):
                window = padded[r * planes + p, pl.ds(start_y, box), :]
                spread_out = jnp.take_along_axis(window, places, axis=1, mode="promise_in_bounds")
                term = spread_out * beta
                totals[r] = term if totals[r] is None else totals[r] + term
        for r in range(rows):
            sums[r, pl.ds(atom, 1), :] = jnp.sum(totals[r], axis=0, keepdims=True)
        return carry

    lax.fori_loop(0, found, one, 0)
    proj_count = lanes // box
    group = lax.broadcasted_iota(jnp.int32, (proj_count, lanes), 1) // box
    member = (group == lax.broadcasted_iota(jnp.int32, (proj_count, lanes), 0)).astype(jnp.float32)
    for r in range(rows):
        coef_ref[r] = lax.dot_general(
            member,
            sums[r],
            (((1,), (1,)), ((), ())),
            precision=highest,
            preferred_element_type=jnp.float32,
        )


def spread_kernel(
    wave_ref,
    potential_ref,
    table_ref,
    coef_ref,
    coupling_ref,
    kinds_ref,
    centres_ref,
    species_ref,
    high_ref,
    low_ref,
    out_ref,
    factors,
    hits,
):
    _, orbitals, planes, extent, _ = wave_ref.shape
    box = table_ref.shape[1]
    lanes = table_ref.shape[2]
    proj_count = lanes // box
    rows = 2 * orbitals
    group = lax.broadcasted_iota(jnp.int32, (proj_count, lanes), 1) // box
    member = (group == lax.broadcasted_iota(jnp.int32, (proj_count, lanes), 0)).astype(jnp.float32)
    kinds = kinds_ref[...]
    for r in range(rows):
        scaled = None
        for s in range(coupling_ref.shape[0]):
            term = jnp.dot(
                coupling_ref[s],
                coef_ref[r],
                precision=highest,
                preferred_element_type=jnp.float32,
            )
            term = jnp.where(kinds == s, term, 0.0)
            scaled = term if scaled is None else scaled + term
        factors[r] = lax.dot_general(
            scaled,
            member,
            (((0,), (0,)), ((), ())),
            precision=highest,
            preferred_element_type=jnp.float32,
        )
    matrix = (high_ref[...], low_ref[...])
    for c in range(2):
        for o in range(orbitals):
            for p in range(planes):
                at = (c * orbitals + o) * planes + p
                value = wave_ref[c, o, p]
                parts = split(value)
                out_ref[at, :extent, :] = (
                    mul(matrix, parts) + mul(parts, matrix) + potential_ref[p] * value
                )
                out_ref[at, extent:, :] = jnp.zeros((box, extent), jnp.float32)
    found = list_hits(centres_ref, hits, extent, planes, box // 2)
    lane = lax.broadcasted_iota(jnp.int32, (box, extent), 1)

    def one(step, carry):
        atom = hits[step]
        slots, start_y, start_z = atom_place(
            centres_ref, species_ref, atom, extent, planes, box
        )
        away = lane - start_z
        inside = jnp.where(away < 0, away + extent, away) < box
        turn = lax.rem(start_z, box)
        factor = [factors[r, pl.ds(atom, 1), :] for r in range(rows)]
        for p in range(planes):
            beta = table_ref[slots[p]]
            for r in range(rows):
                term = beta * factor[r]
                reach = lanes // 2
                while reach >= box:
                    term = term + pltpu.roll(term, reach, 1)
                    reach //= 2
                term = jnp.where(inside, pltpu.roll(term, turn, 1), 0.0)
                out_ref[r * planes + p, pl.ds(start_y, box), :] += term
        return carry

    lax.fori_loop(0, found, one, 0)


def finish_kernel(local_ref, along_ref, out_ref):
    _, orbitals, planes, extent, _ = out_ref.shape
    count = along_ref.shape[0]
    width = extent // count
    box = local_ref.shape[1] - extent
    half_step = 0.5 * time_step
    for c in range(2):
        factor = half_step if c == 1 else -half_step
        for o in range(orbitals):
            r = c * orbitals + o
            for p in range(planes):
                for d in range(count):
                    total = (
                        local_ref[r * planes + p, d * width : (d + 1) * width, :]
                        + along_ref[d, r, pl.ds(p, width, stride=planes), :]
                    )
                    if d * width < box:
                        total += local_ref[
                            r * planes + p, extent + d * width : extent + (d + 1) * width, :
                        ]
                    out_ref[1 - c, o, p, d * width : (d + 1) * width, :] = factor * total


def shape(dims):
    return jax.ShapeDtypeStruct(dims, jnp.float32)


def cost(flops, size):
    return pl.CostEstimate(flops=flops, bytes_accessed=size, transcendentals=0)


def per_device(wave, potential, occupations, centres, species, projectors, coupling):
    _, orbitals, planes, extent, _ = wave.shape
    kind_count, box, proj_count, _ = projectors.shape
    atom_count = species.shape[0]
    count = lax.axis_size("grid")
    rows = 2 * orbitals
    width = extent // count
    lanes = proj_count * box
    size = wave.size * 4
    high, low = second_derivative(extent)
    send, density_term = pl.pallas_call(
        pack_kernel,
        out_shape=(shape((count, rows, width * planes, extent)), shape((planes, extent, extent))),
        in_specs=[VMEM, SMEM],
        out_specs=(VMEM, VMEM),
        compiler_params=params(),
        cost_estimate=cost(wave.size, 2 * size),
        name="pack",
    )(wave, occupations)
    held = lax.all_to_all(send, "grid", 0, 0, tiled=True)
    density = lax.psum_scatter(density_term, "orb", scatter_dimension=1, tiled=True)
    table = projectors.reshape(kind_count, box, proj_count, box, box)
    table = jnp.transpose(table, (0, 1, 3, 2, 4)).reshape(kind_count, box, box, lanes)
    table = jnp.pad(table, ((0, 0), (0, 1), (0, 0), (0, 0)))
    table = table.reshape(kind_count * (box + 1), box, lanes)
    coef = pl.pallas_call(
        project_kernel,
        out_shape=shape((rows, proj_count, atom_count)),
        in_specs=[VMEM, VMEM, SMEM, SMEM],
        out_specs=VMEM,
        scratch_shapes=[
            pltpu.VMEM((rows * planes, extent + box, extent), jnp.float32),
            pltpu.VMEM((rows, atom_count, lanes), jnp.float32),
            pltpu.SMEM((atom_count + 8,), jnp.int32),
        ],
        compiler_params=params(),
        cost_estimate=cost(40 * wave.size, 20 * size),
        name="project",
    )(wave, table, centres, species)
    coef = lax.psum(coef, "grid")
    along = pl.pallas_call(
        along_x_kernel,
        out_shape=shape(held.shape),
        in_specs=[VMEM, VMEM, VMEM],
        out_specs=VMEM,
        scratch_shapes=[pltpu.VMEM((extent, extent), jnp.float32)],
        compiler_params=params(),
        cost_estimate=cost(6 * extent * wave.size, 2 * size),
        name="along_x",
    )(held, high, low)
    back = lax.all_to_all(along, "grid", 0, 0, tiled=True)
    local = pl.pallas_call(
        spread_kernel,
        out_shape=shape((rows * planes, extent + box, extent)),
        in_specs=[VMEM] * 6 + [SMEM, SMEM] + [VMEM] * 2,
        out_specs=VMEM,
        scratch_shapes=[
            pltpu.VMEM((rows, atom_count, lanes), jnp.float32),
            pltpu.SMEM((atom_count + 8,), jnp.int32),
        ],
        compiler_params=params(),
        cost_estimate=cost(40 * wave.size, 20 * size),
        name="spread",
    )(
        wave,
        potential,
        table,
        coef,
        coupling,
        species.reshape(1, atom_count),
        centres,
        species,
        high,
        low,
    )
    update = pl.pallas_call(
        finish_kernel,
        out_shape=shape(wave.shape),
        in_specs=[VMEM, VMEM],
        out_specs=VMEM,
        compiler_params=params(),
        cost_estimate=cost(4 * wave.size, 3 * size),
        name="finish",
    )(local, back)
    return (update, density)


def solution(mesh):
    placed = (
        P(None, "orb", "grid", None, None),
        P("grid", None, None),
        P("orb"),
        P(),
        P(),
        P(),
        P(),
    )
    return jax.shard_map(
        per_device,
        mesh=mesh,
        in_specs=placed,
        out_specs=(P(None, "orb", "grid", None, None), P("grid", "orb", None)),
        check_vma=False,
    )
```

profile of v0, /device:TPU:0, one launch (start us, length us, event | category | flops | bytes accessed | tf_op | source)
XLA Modules:
  0.0 119.0 jit_solution(9800339776041587123)
XLA Ops:
  7.8 0.0 copy-start
  7.8 1.2 %copy-done = f32[2,1,8,128,128]{4,3,2,1,0:T(8,128)S(1)} copy-done((f32[2,1,8,128,128]{4,3,2,1,0:T(8,128)S(1)}, f32[2,1,8,128,128]{4,3,2,1,0:T(8,128)}, u32[]{:S(2)}) %copy-start) | copy-done | bytes 1048600
  9.0 0.0 copy-start.3
  9.0 0.0 copy-start.5
  9.0 1.1 pack.1
  10.2 32.0 %all_to_all.10.held_ref = f32[16,2,64,128]{3,2,1,0:T(8,128)S(1)} all-to-all(f32[16,2,64,128]{3,2,1,0:T(8,128)S(1)} %get-tuple-element.4), channel_id=1, replica_groups=mesh['grid'=16,'orb'=2] {'grid'}, dimensions={0} | all-to-all | bytes 2097152 | tf_op jit(solution)/shard_map/all_to_all | solution.py:291
  42.2 0.0 copy-done.3
  42.2 0.0 copy-done.5
  42.2 0.0 copy-start.13
  42.2 1.5 %along_x.1 = f32[16,2,64,128]{3,2,1,0:T(8,128)} custom-call(f32[16,2,64,128]{3,2,1,0:T(8,128)S(1)} %all_to_all.10.held_ref, bf16[128,128]{1,0:T(8,128)(2,1)S(1)} %copy-done.3, bf16[128,128]{1,0:T(8,128)(2,1)S(1)} %copy-done.5), custom_call_target="tpu_custom_call" | custom-call | flops 201326592 | bytes 2097152 | tf_op jit(solution)/shard_map/along_x/pallas_call | solution.py:312
  43.7 5.0 %all-to-all-start.1 = ((f32[16,2,64,128]{3,2,1,0:T(8,128)}), f32[16,2,64,128]{3,2,1,0:T(8,128)S(1)}, u32[]{:S(2)}, u32[]{:S(2)}) async-start(f32[16,2,64,128]{3,2,1,0:T(8,128)} %along_x.1), calls=%async_computation.1 | async-start | bytes 2097152 | tf_op jit(solution)/shard_map/all_to_all | solution.py:322
  48.7 0.0 reduce-scatter.2.cloned.1.call-start
  48.8 0.7 reduce-scatter.2.cloned.1.call-update
  49.5 0.0 copy-done.13
  49.5 0.6 reshape.16
  50.1 2.2 %copy.11 = f32[2,16,16,8,16]{4,3,2,1,0:T(8,128)} copy(f32[2,16,16,8,16]{4,2,3,1,0:T(8,128)S(1)} %bitcast.10) | data formatting | bytes 524288 | tf_op jit(solution)/shard_map/transpose | solution.py:294
  52.3 0.0 copy-start.1
  52.3 0.0 copy-start.9
  52.3 0.0 copy-start.11
  52.3 2.3 %reshape.17 = f32[2,16,16,128]{3,2,1,0:T(8,128)S(1)} reshape(f32[2,16,16,8,16]{4,3,2,1,0:T(8,128)} %copy.11) | data formatting | bytes 524288 | tf_op jit(solution)/shard_map/reshape | solution.py:294
  54.6 0.0 copy-done.1
  54.6 0.0 copy-done.9
  54.7 0.0 copy-done.11
  54.7 4.6 %project.1 = f32[2,8,128]{2,1,0:T(8,128)S(1)} custom-call(f32[2,1,8,128,128]{4,3,2,1,0:T(8,128)S(1)} %copy-done.1, f32[34,16,128]{2,1,0:T(8,128)S(1)} %bitcast.7, s32[3,128]{1,0:T(4,128)S(1)} %copy-done.9, s32[128]{0:T(128)S(1)} %copy-done.11), custom_call_target="tpu_custom_call" | custom-call | flops 10485760 | bytes 20971520 | tf_op jit(solution)/shard_map/project/pallas_call | solution.py:297
  59.3 35.8 %psum.7.coef_ref = f32[2,8,128]{2,1,0:T(8,128)} all-reduce(f32[2,8,128]{2,1,0:T(8,128)S(1)} %project.1), channel_id=1, replica_groups=mesh['grid'=16,'orb'=2] {'grid'}, use_global_device_ids=true, to_apply=%region_0.0 | all-reduce | flops 2048 | bytes 16384 | tf_op jit(solution)/shard_map/psum | solution.py:311
  95.1 0.0 copy-start.2
  95.1 1.0 copy-done.2
  96.1 0.0 copy-start.4
  96.1 0.8 copy-done.4
  96.9 0.0 copy-start.6
  96.9 0.8 copy-done.6
  97.6 0.0 copy-start.7
  97.6 0.7 copy-done.7
  98.3 0.0 copy-start.8
  98.3 0.7 copy-done.8
  99.0 0.0 copy-start.10
  99.0 0.7 copy-done.10
  99.7 0.0 copy-start.12
  99.7 0.7 copy-done.12
  100.4 10.5 %spread.1.local_ref = f32[16,144,128]{2,1,0:T(8,128)S(1)} custom-call(f32[2,1,8,128,128]{4,3,2,1,0:T(8,128)S(1)} %copy-done.1, f32[8,128,128]{2,1,0:T(8,128)S(1)} %copy-done.2, f32[34,16,128]{2,1,0:T(8,128)S(1)} %bitcast.8, f32[2,8,128]{2,1,0:T(8,128)S(1)} %copy-done.7, f32[2,8,8]{2,1,0:T(8,128)S(1)} %copy-done.8, s32[1,128]{1,0:T(1,128)S(1)} %bitcast.9, ...), custom_call_target="tpu_custom_call" | custom-call | flops 10485760 | bytes 20971520 | tf_op jit(solution)/shard_map/spread/pallas_call | solution.py:323
  110.9 0.0 all-to-all-done.1.along_ref
  110.9 1.2 %finish.1 = f32[2,1,8,128,128]{4,3,2,1,0:T(8,128)} custom-call(f32[16,144,128]{2,1,0:T(8,128)S(1)} %spread.1.local_ref, f32[16,2,64,128]{3,2,1,0:T(8,128)S(1)} %all-to-all-done.1.along_ref), custom_call_target="tpu_custom_call" | custom-call | flops 1048576 | bytes 3145728 | tf_op jit(solution)/shard_map/finish/pallas_call | solution.py:347
  112.2 0.0 reduce-scatter.2.cloned.1.call-done
  (1 shorter events, 0.0 us)
Async XLA Ops:
  7.8 1.2 %copy-start = (f32[2,1,8,128,128]{4,3,2,1,0:T(8,128)S(1)}, f32[2,1,8,128,128]{4,3,2,1,0:T(8,128)}, u32[]{:S(2)}) copy-start(f32[2,1,8,128,128]{4,3,2,1,0:T(8,128)} %wave_ref.5) | copy-start | bytes 3145732
  9.0 33.1 %copy-start.3 = (bf16[128,128]{1,0:T(8,128)(2,1)S(1)}, bf16[128,128]{1,0:T(8,128)(2,1)}, u32[]{:S(2)}) copy-start(bf16[128,128]{1,0:T(8,128)(2,1)} %constant.7.clone.high_ref) | copy-start | bytes 98308
  9.0 33.1 %copy-start.5 = (bf16[128,128]{1,0:T(8,128)(2,1)S(1)}, bf16[128,128]{1,0:T(8,128)(2,1)}, u32[]{:S(2)}) copy-start(bf16[128,128]{1,0:T(8,128)(2,1)} %constant.8.clone.low_ref) | copy-start | bytes 98308
  42.2 7.3 %copy-start.13 = (f32[2,16,8,256]{3,2,1,0:T(8,128)S(1)}, f32[2,16,8,256]{3,2,1,0:T(8,128)}, u32[]{:S(2)}) copy-start(f32[2,16,8,256]{3,2,1,0:T(8,128)} %param.14) | copy-start | bytes 786436
  43.7 67.2 %all-to-all-start.1 = ((f32[16,2,64,128]{3,2,1,0:T(8,128)}), f32[16,2,64,128]{3,2,1,0:T(8,128)S(1)}, u32[]{:S(2)}, u32[]{:S(2)}) async-start(f32[16,2,64,128]{3,2,1,0:T(8,128)} %along_x.1), calls=%async_computation.1 | async-start | bytes 2097152 | tf_op jit(solution)/shard_map/all_to_all | solution.py:322
  48.7 63.4 %reduce-scatter.2.cloned.1.call-start = ((), (), s32[]{:S(2)}) async-start(), calls=%async_computation.3 | async-start | bytes 786432 | tf_op jit(solution)/shard_map/reduce_scatter | solution.py:292
  52.3 2.3 %copy-start.1 = (f32[2,1,8,128,128]{4,3,2,1,0:T(8,128)S(1)}, f32[2,1,8,128,128]{4,3,2,1,0:T(8,128)}, u32[]{:S(2)}) copy-start(f32[2,1,8,128,128]{4,3,2,1,0:T(8,128)} %wave_ref.5) | copy-start | bytes 3145732
  52.3 2.3 %copy-start.9 = (s32[3,128]{1,0:T(4,128)S(1)}, s32[3,128]{1,0:T(4,128)}, u32[]{:S(2)}) copy-start(s32[3,128]{1,0:T(4,128)} %centres_ref.3) | copy-start | bytes 4612
  52.3 2.3 %copy-start.11 = (s32[128]{0:T(128)S(1)}, s32[128]{0:T(128)}, u32[]{:S(2)}) copy-start(s32[128]{0:T(128)} %species_ref.3) | copy-start | bytes 1540
  95.1 1.0 copy-start.2
  96.1 0.8 copy-start.4
  96.9 0.8 copy-start.6
  97.6 0.7 copy-start.7
  98.3 0.7 copy-start.8
  99.0 0.7 copy-start.10
  99.7 0.7 copy-start.12
Sparse Core Ops, SparseCore 0:
  52.4 15.9 reduce-scatter.1
where the time goes:
time: 119 us
  blocking collectives  67.8 us (57%)
  Pallas kernels  19.1 us (16%)
  between operations  14.8 us (12%)
  local copies, waits for them, and re-layouts  11.7 us (10%)
  starting transfers between devices  5.03 us (4%)
    psum x1, blocking collectives, per_device(): coef = lax.psum(coef, 'grid')  35.8 us
    all_to_all x1, blocking collectives, per_device(): held = lax.all_to_all(send, 'grid', 0, 0, tiled=True)  32 us
    pallas_call x1, Pallas kernels, per_device(): pl.pallas_call(spread_kernel, out_shape=shape((rows * planes, extent + bo...  10.5 us
    unnamed x28, local copies, waits for them, and re-layouts  6.53 us
    all_to_all x1, starting transfers between devices, per_device(): back = lax.all_to_all(along, 'grid', 0, 0, tiled=True)  4.99 us
    pallas_call x1, Pallas kernels, per_device(): pl.pallas_call(project_kernel, out_shape=shape((rows, proj_count, atom_co...  4.64 us
  transfers between devices with their start and end apart: 2, of which 0 were waited for; matrix products, arithmetic and copies ran while one was open for 4% of the time, Pallas kernels for 14%

commit v1 on v0

--- a/solution.py
+++ b/solution.py
@@ -13,6 +13,12 @@
 highest = lax.Precision.HIGHEST
 VMEM = pl.BlockSpec(memory_space=pltpu.VMEM)
 SMEM = pl.BlockSpec(memory_space=pltpu.SMEM)
+
+
+def passed_along(value, steps):
+    count = lax.axis_size("grid")
+    pairs = [(source, (source + steps) % count) for source in range(count)]
+    return lax.ppermute(value, "grid", pairs)
 
 
 def params():
@@ -28,7 +34,7 @@
     full = row[(counts[:, None] - counts[None, :]) % extent].astype(np.float32)
     high = full.astype(jnp.bfloat16)
     low = (full - high.astype(np.float32)).astype(jnp.bfloat16)
-    return jnp.asarray(high), jnp.asarray(low)
+    return jnp.asarray(np.stack([high, low]))
 
 
 def split(value):
@@ -64,10 +70,10 @@
                     ]
 
 
-def along_x_kernel(held_ref, high_ref, low_ref, out_ref, lined):
+def along_x_kernel(held_ref, matrix_ref, coef_ref, out_ref, lined):
     count, rows, both, extent = held_ref.shape
     planes = extent // count
-    matrix = (high_ref[...], low_ref[...])
+    matrix = (matrix_ref[0], matrix_ref[1])
     for r in range(rows):
         for y in range(both // planes):
             block = pl.ds(y * planes, planes)
@@ -111,7 +117,18 @@
     return slots, start_y, start_z
 
 
-def project_kernel(wave_ref, table_ref, centres_ref, species_ref, coef_ref, padded, sums, hits):
+def project_kernel(
+    wave_ref,
+    table_ref,
+    coupling_ref,
+    kinds_ref,
+    centres_ref,
+    species_ref,
+    coef_ref,
+    padded,
+    sums,
+    hits,
+):
     _, orbitals, planes, extent, _ = wave_ref.shape
     box = table_ref.shape[1]
     lanes = table_ref.shape[2]
@@ -149,58 +166,29 @@
     proj_count = lanes // box
     group = lax.broadcasted_iota(jnp.int32, (proj_count, lanes), 1) // box
     member = (group == lax.broadcasted_iota(jnp.int32, (proj_count, lanes), 0)).astype(jnp.float32)
+    kinds = kinds_ref[...]
     for r in range(rows):
-        coef_ref[r] = lax.dot_general(
+        partial = lax.dot_general(
             member,
             sums[r],
             (((1,), (1,)), ((), ())),
             precision=highest,
             preferred_element_type=jnp.float32,
         )
-
-
-def spread_kernel(
-    wave_ref,
-    potential_ref,
-    table_ref,
-    coef_ref,
-    coupling_ref,
-    kinds_ref,
-    centres_ref,
-    species_ref,
-    high_ref,
-    low_ref,
-    out_ref,
-    factors,
-    hits,
-):
-    _, orbitals, planes, extent, _ = wave_ref.shape
-    box = table_ref.shape[1]
-    lanes = table_ref.shape[2]
-    proj_count = lanes // box
-    rows = 2 * orbitals
-    group = lax.broadcasted_iota(jnp.int32, (proj_count, lanes), 1) // box
-    member = (group == lax.broadcasted_iota(jnp.int32, (proj_count, lanes), 0)).astype(jnp.float32)
-    kinds = kinds_ref[...]
-    for r in range(rows):
         scaled = None
         for s in range(coupling_ref.shape[0]):
             term = jnp.dot(
-                coupling_ref[s],
-                coef_ref[r],
-                precision=highest,
-                preferred_element_type=jnp.float32,
+                coupling_ref[s], partial, precision=highest, preferred_element_type=jnp.float32
             )
             term = jnp.where(kinds == s, term, 0.0)
             scaled = term if scaled is None else scaled + term
-        factors[r] = lax.dot_general(
-            scaled,
-            member,
-            (((0,), (0,)), ((), ())),
-            precision=highest,
-            preferred_element_type=jnp.float32,
-        )
-    matrix = (high_ref[...], low_ref[...])
+        coef_ref[r] = scaled
+
+
+def local_kernel(wave_ref, potential_ref, matrix_ref, out_ref):
+    _, orbitals, planes, extent, _ = wave_ref.shape
+    box = out_ref.shape[1] - extent
+    matrix = (matrix_ref[0], matrix_ref[1])
     for c in range(2):
         for o in range(orbitals):
             for p in range(planes):
@@ -211,6 +199,26 @@
                     mul(matrix, parts) + mul(parts, matrix) + potential_ref[p] * value
                 )
                 out_ref[at, extent:, :] = jnp.zeros((box, extent), jnp.float32)
+
+
+def spread_kernel(local_ref, table_ref, coef_ref, centres_ref, species_ref, out_ref, factors, hits):
+    box = table_ref.shape[1]
+    lanes = table_ref.shape[2]
+    extent = local_ref.shape[2]
+    rows = coef_ref.shape[0]
+    planes = local_ref.shape[0] // rows
+    proj_count = lanes // box
+    group = lax.broadcasted_iota(jnp.int32, (proj_count, lanes), 1) // box
+    member = (group == lax.broadcasted_iota(jnp.int32, (proj_count, lanes), 0)).astype(jnp.float32)
+    for r in range(rows):
+        factors[r] = lax.dot_general(
+            coef_ref[r],
+            member,
+            (((0,), (0,)), ((), ())),
+            precision=highest,
+            preferred_element_type=jnp.float32,
+        )
+    out_ref[...] = local_ref[...]
     found = list_hits(centres_ref, hits, extent, planes, box // 2)
     lane = lax.broadcasted_iota(jnp.int32, (box, extent), 1)
 
@@ -278,7 +286,8 @@
     width = extent // count
     lanes = proj_count * box
     size = wave.size * 4
-    high, low = second_derivative(extent)
+    matrix = second_derivative(extent)
+    kinds = species.reshape(1, atom_count)
     send, density_term = pl.pallas_call(
         pack_kernel,
         out_shape=(shape((count, rows, width * planes, extent)), shape((planes, extent, extent))),
@@ -297,7 +306,7 @@
     coef = pl.pallas_call(
         project_kernel,
         out_shape=shape((rows, proj_count, atom_count)),
-        in_specs=[VMEM, VMEM, SMEM, SMEM],
+        in_specs=[VMEM] * 4 + [SMEM] * 2,
         out_specs=VMEM,
         scratch_shapes=[
             pltpu.VMEM((rows * planes, extent + box, extent), jnp.float32),
@@ -307,23 +316,33 @@
         compiler_params=params(),
         cost_estimate=cost(40 * wave.size, 20 * size),
         name="project",
-    )(wave, table, centres, species)
-    coef = lax.psum(coef, "grid")
+    )(wave, table, coupling, kinds, centres, species)
+    reach = (box + planes - 2) // planes
+    coef = coef + sum(passed_along(coef, step) for hop in range(reach) for step in (hop + 1, -hop - 1))
+    local = pl.pallas_call(
+        local_kernel,
+        out_shape=shape((rows * planes, extent + box, extent)),
+        in_specs=[VMEM] * 3,
+        out_specs=VMEM,
+        compiler_params=params(),
+        cost_estimate=cost(12 * extent * wave.size, 3 * size),
+        name="local",
+    )(wave, potential, matrix)
     along = pl.pallas_call(
         along_x_kernel,
         out_shape=shape(held.shape),
-        in_specs=[VMEM, VMEM, VMEM],
+        in_specs=[VMEM, VMEM, pl.BlockSpec(memory_space=pl.ANY)],
         out_specs=VMEM,
         scratch_shapes=[pltpu.VMEM((extent, extent), jnp.float32)],
         compiler_params=params(),
         cost_estimate=cost(6 * extent * wave.size, 2 * size),
         name="along_x",
-    )(held, high, low)
+    )(held, matrix, coef)
     back = lax.all_to_all(along, "grid", 0, 0, tiled=True)
     local = pl.pallas_call(
         spread_kernel,
-        out_shape=shape((rows * planes, extent + box, extent)),
-        in_specs=[VMEM] * 6 + [SMEM, SMEM] + [VMEM] * 2,
+        out_shape=shape(local.shape),
+        in_specs=[VMEM] * 3 + [SMEM] * 2,
         out_specs=VMEM,
         scratch_shapes=[
             pltpu.VMEM((rows, atom_count, lanes), jnp.float32),
@@ -332,18 +351,7 @@
         compiler_params=params(),
         cost_estimate=cost(40 * wave.size, 20 * size),
         name="spread",
-    )(
-        wave,
-        potential,
-        table,
-        coef,
-        coupling,
-        species.reshape(1, atom_count),
-        centres,
-        species,
-        high,
-        low,
-    )
+    )(local, table, coef, centres, species)
     update = pl.pallas_call(
         finish_kernel,
         out_shape=shape(wave.shape),

time: 119 us -> 82.2 us (0.69)
  the two profiles are of different devices: /device:TPU:0 before, /device:TPU:16 now
where the time goes in v1:
time: 82.2 us; the launch traced here: 81.7 us
  Pallas kernels  26.5 us (32%)
  starting transfers between devices  16.6 us (20%)
  between operations  14.8 us (18%)
  waiting for transfers between devices  14.5 us (18%)
  local copies, waits for them, and re-layouts  9.33 us (11%)
    pallas_call x1, Pallas kernels, per_device(): pl.pallas_call(spread_kernel, out_shape=shape(local.shape), in_specs=[VME...  14.4 us
    all_to_all x1, waiting for transfers between devices, per_device(): back = lax.all_to_all(along, 'grid', 0, 0, tiled=True)  9.09 us
    pallas_call x1, Pallas kernels, per_device(): pl.pallas_call(project_kernel, out_shape=shape((rows, proj_count, atom_co...  6.94 us
    all_to_all x1, starting transfers between devices, per_device(): held = lax.all_to_all(send, 'grid', 0, 0, tiled=True)  6.16 us
    ppermute x4, starting transfers between devices, passed_along(): return lax.ppermute(value, 'grid', pairs)  5.59 us
    all_to_all x1, starting transfers between devices, per_device(): back = lax.all_to_all(along, 'grid', 0, 0, tiled=True)  4.77 us
    ppermute x4, waiting for transfers between devices, passed_along(): return lax.ppermute(value, 'grid', pairs)  4.75 us
    transpose x1, local copies, waits for them, and re-layouts, per_device(): jnp.transpose(table, (0, 1, 3, 2, 4)).reshape(kind_count, box, box, lanes)  3.79 us
  transfers between devices with their start and end apart: 7, of which 3 were waited for; matrix products, arithmetic and copies ran while one was open for 10% of the time, Pallas kernels for 29%

profile of v1, /device:TPU:16, one launch (start us, length us, event | category | flops | bytes accessed | tf_op | source)
XLA Modules:
  0.0 81.7 jit_solution(1643045711638277625)
XLA Ops:
  7.8 0.0 copy-start
  7.8 1.2 %copy-done = f32[2,1,8,128,128]{4,3,2,1,0:T(8,128)S(1)} copy-done((f32[2,1,8,128,128]{4,3,2,1,0:T(8,128)S(1)}, f32[2,1,8,128,128]{4,3,2,1,0:T(8,128)}, u32[]{:S(2)}) %copy-start) | copy-done | bytes 1048600
  9.0 0.0 copy-start.7
  9.0 1.5 %pack.1 = (f32[16,2,64,128]{3,2,1,0:T(8,128)}, f32[8,128,128]{2,1,0:T(8,128)}) custom-call(f32[2,1,8,128,128]{4,3,2,1,0:T(8,128)S(1)} %copy-done, f32[1]{0:T(128)S(6)} %copy.11.occ_ref), custom_call_target="tpu_custom_call" | custom-call | flops 262144 | bytes 2097152 | tf_op jit(solution)/shard_map/pack/pallas_call | solution.py:291
  10.5 6.2 %all-to-all-start = ((f32[16,2,64,128]{3,2,1,0:T(8,128)}), f32[16,2,64,128]{3,2,1,0:T(8,128)S(1)}, u32[]{:S(2)}, u32[]{:S(2)}) async-start(f32[16,2,64,128]{3,2,1,0:T(8,128)} %get-tuple-element.4), calls=%async_computation | async-start | bytes 2097152 | tf_op jit(solution)/shard_map/all_to_all | solution.py:300
  16.7 0.0 copy-done.7
  16.7 2.0 %reshape.16 = f32[2,16,8,16,16]{4,3,2,1,0:T(8,128)} reshape(f32[2,16,8,256]{3,2,1,0:T(8,128)S(1)} %copy-done.7) | data formatting | bytes 524288 | tf_op jit(solution)/shard_map/reshape | solution.py:302
  18.7 3.8 %copy.10 = f32[2,16,16,8,16]{4,3,2,1,0:T(8,128)} copy(f32[2,16,16,8,16]{4,2,3,1,0:T(8,128)} %bitcast.10) | data formatting | bytes 524288 | tf_op jit(solution)/shard_map/transpose | solution.py:303
  22.5 0.0 copy-start.1
  22.5 0.0 copy-start.4
  22.5 0.0 copy-start.5
  22.5 0.0 copy-start.6
  22.5 0.0 copy-start.3
  22.5 2.3 %reshape.17 = f32[2,16,16,128]{3,2,1,0:T(8,128)S(1)} reshape(f32[2,16,16,8,16]{4,3,2,1,0:T(8,128)} %copy.10) | data formatting | bytes 524288 | tf_op jit(solution)/shard_map/reshape | solution.py:303
  24.8 0.0 copy-done.1
  24.8 0.0 copy-done.4
  24.8 0.0 copy-done.5
  24.8 0.0 copy-done.6
  24.8 6.9 %project.1 = f32[2,8,128]{2,1,0:T(8,128)S(1)} custom-call(f32[2,1,8,128,128]{4,3,2,1,0:T(8,128)S(1)} %copy-done.1, f32[34,16,128]{2,1,0:T(8,128)S(1)} %bitcast.7, f32[2,8,8]{2,1,0:T(8,128)S(1)} %copy-done.4, s32[1,128]{1,0:T(1,128)S(1)} %bitcast.9, s32[3,128]{1,0:T(4,128)S(1)} %copy-done.5, s32[128]{0:T(128)S(1)} %copy-done.6), custom_call_target="tpu_custom_call" | custom-call | flops 10485760 | bytes 20971520 | tf_op jit(solution)/shard_map/project/pallas_call | solution.py:306
  31.8 0.0 collective-permute-start
  31.8 2.7 %collective-permute-start.1 = (f32[2,8,128]{2,1,0:T(8,128)S(1)}, f32[2,8,128]{2,1,0:T(8,128)S(1)}, u32[]{:S(2)}, u32[]{:S(2)}) collective-permute-start(f32[2,8,128]{2,1,0:T(8,128)S(1)} %project.1), channel_id=1, source_target_pairs={{0,30},{2,0},{4,2},{6,4},{8,6},{10,8},{12,10},{14,12},{16,14},{18,... | collective-permute-start | bytes 24584 | tf_op jit(solution)/shard_map/ppermute | solution.py:21
  34.4 0.0 collective-permute-start.2
  34.4 2.9 %collective-permute-start.3 = (f32[2,8,128]{2,1,0:T(8,128)S(1)}, f32[2,8,128]{2,1,0:T(8,128)S(1)}, u32[]{:S(2)}, u32[]{:S(2)}) collective-permute-start(f32[2,8,128]{2,1,0:T(8,128)S(1)} %project.1), channel_id=1, source_target_pairs={{0,28},{2,30},{4,0},{6,2},{8,4},{10,6},{12,8},{14,10},{16,12},{18,... | collective-permute-start | bytes 24584 | tf_op jit(solution)/shard_map/ppermute | solution.py:21
  37.4 4.2 %collective-permute-done = f32[2,8,128]{2,1,0:T(8,128)S(1)} collective-permute-done((f32[2,8,128]{2,1,0:T(8,128)S(1)}, f32[2,8,128]{2,1,0:T(8,128)S(1)}, u32[]{:S(2)}, u32[]{:S(2)}) %collective-permute-start) | collective-permute-done | bytes 8224 | tf_op jit(solution)/shard_map/ppermute | solution.py:21
  41.5 0.0 collective-permute-done.1
  41.5 0.6 collective-permute-done.2
  42.1 0.0 collective-permute-done.3
  42.1 0.0 copy-start.2
  42.1 0.0 all-to-all-done.held_ref
  42.1 0.0 copy-done.3
  42.2 1.5 %along_x.1 = f32[16,2,64,128]{3,2,1,0:T(8,128)} custom-call(f32[16,2,64,128]{3,2,1,0:T(8,128)S(1)} %all-to-all-done.held_ref, bf16[2,128,128]{2,1,0:T(8,128)(2,1)S(1)} %copy-done.3, f32[2,8,128]{2,1,0:T(8,128)S(1)} %add_add_fusion.coef_ref), custom_call_target="tpu_custom_call" | custom-call | flops 201326592 | bytes 2097152 | tf_op jit(solution)/shard_map/along_x/pallas_call | solution.py:331
  43.7 4.8 %all-to-all-start.1 = ((f32[16,2,64,128]{3,2,1,0:T(8,128)}), f32[16,2,64,128]{3,2,1,0:T(8,128)S(1)}, u32[]{:S(2)}, u32[]{:S(2)}) async-start(f32[16,2,64,128]{3,2,1,0:T(8,128)} %along_x.1), calls=%async_computation.1 | async-start | bytes 2097152 | tf_op jit(solution)/shard_map/all_to_all | solution.py:341
  48.5 0.0 reduce-scatter.2.cloned.1.call-start
  48.5 0.7 reduce-scatter.2.cloned.1.call-update
  49.2 0.0 copy-done.2
  49.2 1.0 %local.1.local_ref = f32[16,144,128]{2,1,0:T(8,128)S(1)} custom-call(f32[2,1,8,128,128]{4,3,2,1,0:T(8,128)S(1)} %copy-done.1, f32[8,128,128]{2,1,0:T(8,128)S(1)} %copy-done.2, bf16[2,128,128]{2,1,0:T(8,128)(2,1)S(1)} %copy-done.3), custom_call_target="tpu_custom_call" | custom-call | flops 402653184 | bytes 3145728 | tf_op jit(solution)/shard_map/local/pallas_call | solution.py:322
  50.2 14.4 %spread.1.local_ref = f32[16,144,128]{2,1,0:T(8,128)S(1)} custom-call(f32[16,144,128]{2,1,0:T(8,128)S(1)} %local.1.local_ref, f32[34,16,128]{2,1,0:T(8,128)S(1)} %bitcast.8, f32[2,8,128]{2,1,0:T(8,128)S(1)} %add_add_fusion.coef_ref, s32[3,128]{1,0:T(4,128)S(1)} %copy-done.5, s32[128]{0:T(128)S(1)} %copy-done.6), custom_call_target="tpu_custom_call" | custom-call | flops 10485760 | bytes 20971520 | tf_op jit(solution)/shard_map/spread/pallas_call | solution.py:342
  64.5 9.1 %all-to-all-done.1.along_ref = f32[16,2,64,128]{3,2,1,0:T(8,128)S(1)} async-done(((f32[16,2,64,128]{3,2,1,0:T(8,128)}), f32[16,2,64,128]{3,2,1,0:T(8,128)S(1)}, u32[]{:S(2)}, u32[]{:S(2)}) %all-to-all-start.1) | async-done | bytes 1048608 | tf_op jit(solution)/shard_map/all_to_all | solution.py:341
  73.6 1.2 %finish.1 = f32[2,1,8,128,128]{4,3,2,1,0:T(8,128)} custom-call(f32[16,144,128]{2,1,0:T(8,128)S(1)} %spread.1.local_ref, f32[16,2,64,128]{3,2,1,0:T(8,128)S(1)} %all-to-all-done.1.along_ref), custom_call_target="tpu_custom_call" | custom-call | flops 1048576 | bytes 3145728 | tf_op jit(solution)/shard_map/finish/pallas_call | solution.py:355
  74.9 0.0 reduce-scatter.2.cloned.1.call-done
  (2 shorter events, 0.0 us)
Async XLA Ops:
  7.8 1.2 %copy-start = (f32[2,1,8,128,128]{4,3,2,1,0:T(8,128)S(1)}, f32[2,1,8,128,128]{4,3,2,1,0:T(8,128)}, u32[]{:S(2)}) copy-start(f32[2,1,8,128,128]{4,3,2,1,0:T(8,128)} %wave_ref.5) | copy-start | bytes 3145732
  9.0 7.6 %copy-start.7 = (f32[2,16,8,256]{3,2,1,0:T(8,128)S(1)}, f32[2,16,8,256]{3,2,1,0:T(8,128)}, u32[]{:S(2)}) copy-start(f32[2,16,8,256]{3,2,1,0:T(8,128)} %param.13) | copy-start | bytes 786436
  10.5 31.6 %all-to-all-start = ((f32[16,2,64,128]{3,2,1,0:T(8,128)}), f32[16,2,64,128]{3,2,1,0:T(8,128)S(1)}, u32[]{:S(2)}, u32[]{:S(2)}) async-start(f32[16,2,64,128]{3,2,1,0:T(8,128)} %get-tuple-element.4), calls=%async_computation | async-start | bytes 2097152 | tf_op jit(solution)/shard_map/all_to_all | solution.py:300
  22.5 2.3 %copy-start.1 = (f32[2,1,8,128,128]{4,3,2,1,0:T(8,128)S(1)}, f32[2,1,8,128,128]{4,3,2,1,0:T(8,128)}, u32[]{:S(2)}) copy-start(f32[2,1,8,128,128]{4,3,2,1,0:T(8,128)} %wave_ref.5) | copy-start | bytes 3145732
  22.5 2.3 %copy-start.4 = (f32[2,8,8]{2,1,0:T(8,128)S(1)}, f32[2,8,8]{2,1,0:T(8,128)}, u32[]{:S(2)}) copy-start(f32[2,8,8]{2,1,0:T(8,128)} %coupling_ref.1) | copy-start | bytes 1540
  22.5 2.3 %copy-start.5 = (s32[3,128]{1,0:T(4,128)S(1)}, s32[3,128]{1,0:T(4,128)}, u32[]{:S(2)}) copy-start(s32[3,128]{1,0:T(4,128)} %centres_ref.3) | copy-start | bytes 4612
  22.5 2.3 %copy-start.6 = (s32[128]{0:T(128)S(1)}, s32[128]{0:T(128)}, u32[]{:S(2)}) copy-start(s32[128]{0:T(128)} %species_ref.3) | copy-start | bytes 1540
  22.5 19.7 %copy-start.3 = (bf16[2,128,128]{2,1,0:T(8,128)(2,1)S(1)}, bf16[2,128,128]{2,1,0:T(8,128)(2,1)}, u32[]{:S(2)}) copy-start(bf16[2,128,128]{2,1,0:T(8,128)(2,1)} %constant.5.clone.matrix_ref) | copy-start | bytes 196612
  31.8 9.8 %collective-permute-start = (f32[2,8,128]{2,1,0:T(8,128)S(1)}, f32[2,8,128]{2,1,0:T(8,128)S(1)}, u32[]{:S(2)}, u32[]{:S(2)}) collective-permute-start(f32[2,8,128]{2,1,0:T(8,128)S(1)} %project.1), channel_id=1, source_target_pairs={{0,2},{2,4},{4,6},{6,8},{8,10},{10,12},{12,14},{14,16},{16,18},{18... | collective-permute-start | bytes 24584 | tf_op jit(solution)/shard_map/ppermute | solution.py:21
  31.8 9.8 %collective-permute-start.1 = (f32[2,8,128]{2,1,0:T(8,128)S(1)}, f32[2,8,128]{2,1,0:T(8,128)S(1)}, u32[]{:S(2)}, u32[]{:S(2)}) collective-permute-start(f32[2,8,128]{2,1,0:T(8,128)S(1)} %project.1), channel_id=1, source_target_pairs={{0,30},{2,0},{4,2},{6,4},{8,6},{10,8},{12,10},{14,12},{16,14},{18,... | collective-permute-start | bytes 24584 | tf_op jit(solution)/shard_map/ppermute | solution.py:21
  34.4 7.7 %collective-permute-start.2 = (f32[2,8,128]{2,1,0:T(8,128)S(1)}, f32[2,8,128]{2,1,0:T(8,128)S(1)}, u32[]{:S(2)}, u32[]{:S(2)}) collective-permute-start(f32[2,8,128]{2,1,0:T(8,128)S(1)} %project.1), channel_id=1, source_target_pairs={{0,4},{2,6},{4,8},{6,10},{8,12},{10,14},{12,16},{14,18},{16,20},{1... | collective-permute-start | bytes 24584 | tf_op jit(solution)/shard_map/ppermute | solution.py:21
  34.4 7.7 %collective-permute-start.3 = (f32[2,8,128]{2,1,0:T(8,128)S(1)}, f32[2,8,128]{2,1,0:T(8,128)S(1)}, u32[]{:S(2)}, u32[]{:S(2)}) collective-permute-start(f32[2,8,128]{2,1,0:T(8,128)S(1)} %project.1), channel_id=1, source_target_pairs={{0,28},{2,30},{4,0},{6,2},{8,4},{10,6},{12,8},{14,10},{16,12},{18,... | collective-permute-start | bytes 24584 | tf_op jit(solution)/shard_map/ppermute | solution.py:21
  42.1 7.1 %copy-start.2 = (f32[8,128,128]{2,1,0:T(8,128)S(1)}, f32[8,128,128]{2,1,0:T(8,128)}, u32[]{:S(2)}) copy-start(f32[8,128,128]{2,1,0:T(8,128)} %potential_ref.1) | copy-start | bytes 1572868
  43.7 29.9 %all-to-all-start.1 = ((f32[16,2,64,128]{3,2,1,0:T(8,128)}), f32[16,2,64,128]{3,2,1,0:T(8,128)S(1)}, u32[]{:S(2)}, u32[]{:S(2)}) async-start(f32[16,2,64,128]{3,2,1,0:T(8,128)} %along_x.1), calls=%async_computation.1 | async-start | bytes 2097152 | tf_op jit(solution)/shard_map/all_to_all | solution.py:341
  48.5 26.4 %reduce-scatter.2.cloned.1.call-start = ((), (), s32[]{:S(2)}) async-start(), calls=%async_computation.3 | async-start | bytes 786432 | tf_op jit(solution)/shard_map/reduce_scatter | solution.py:301
Sparse Core Ops, SparseCore 0:
  52.1 15.5 reduce-scatter.1

commit v2 on v1

--- a/solution.py
+++ b/solution.py
@@ -15,10 +15,10 @@
 SMEM = pl.BlockSpec(memory_space=pltpu.SMEM)
 
 
-def passed_along(value, steps):
-    count = lax.axis_size("grid")
+def passed_along(value, axis, steps):
+    count = lax.axis_size(axis)
     pairs = [(source, (source + steps) % count) for source in range(count)]
-    return lax.ppermute(value, "grid", pairs)
+    return lax.ppermute(value, axis, pairs)
 
 
 def params():
@@ -50,18 +50,23 @@
     return dot(left[0], right[0]) + (dot(left[0], right[1]) + dot(left[1], right[0]))
 
 
-def pack_kernel(wave_ref, occ_ref, send_ref, density_ref):
+def pack_kernel(wave_ref, occ_ref, send_ref, *density_refs):
     _, orbitals, planes, extent, _ = wave_ref.shape
     count = send_ref.shape[0]
     width = extent // count
+    shares = len(density_refs)
+    share = extent // shares
+    place = lax.axis_index("orb")
     for p in range(planes):
-        total = None
-        for o in range(orbitals):
-            real = wave_ref[0, o, p]
-            imag = wave_ref[1, o, p]
-            term = occ_ref[o] * (real * real + imag * imag)
-            total = term if total is None else total + term
-        density_ref[p] = total
+        for k in range(shares):
+            taken = pl.ds(pl.multiple_of(lax.rem(place + k, shares) * share, share), share)
+            total = None
+            for o in range(orbitals):
+                real = wave_ref[0, o, p, taken, :]
+                imag = wave_ref[1, o, p, taken, :]
+                term = occ_ref[o] * (real * real + imag * imag)
+                total = term if total is None else total + term
+            density_refs[k][p] = total
         for c in range(2):
             for o in range(orbitals):
                 for d in range(count):
@@ -246,11 +251,16 @@
     lax.fori_loop(0, found, one, 0)
 
 
-def finish_kernel(local_ref, along_ref, out_ref):
+def finish_kernel(local_ref, along_ref, *refs):
+    terms, out_ref, density_ref = refs[:-2], refs[-2], refs[-1]
     _, orbitals, planes, extent, _ = out_ref.shape
     count = along_ref.shape[0]
     width = extent // count
     box = local_ref.shape[1] - extent
+    density = terms[0][...]
+    for term in terms[1:]:
+        density = density + term[...]
+    density_ref[...] = density
     half_step = 0.5 * time_step
     for c in range(2):
         factor = half_step if c == 1 else -half_step
@@ -288,17 +298,19 @@
     size = wave.size * 4
     matrix = second_derivative(extent)
     kinds = species.reshape(1, atom_count)
-    send, density_term = pl.pallas_call(
+    shares = lax.axis_size("orb")
+    density_shape = shape((planes, extent // shares, extent))
+    send, *terms = pl.pallas_call(
         pack_kernel,
-        out_shape=(shape((count, rows, width * planes, extent)), shape((planes, extent, extent))),
+        out_shape=[shape((count, rows, width * planes, extent))] + [density_shape] * shares,
         in_specs=[VMEM, SMEM],
-        out_specs=(VMEM, VMEM),
+        out_specs=[VMEM] * (shares + 1),
         compiler_params=params(),
         cost_estimate=cost(wave.size, 2 * size),
         name="pack",
     )(wave, occupations)
     held = lax.all_to_all(send, "grid", 0, 0, tiled=True)
-    density = lax.psum_scatter(density_term, "orb", scatter_dimension=1, tiled=True)
+    terms = [terms[0]] + [passed_along(terms[k], "orb", k) for k in range(1, shares)]
     table = projectors.reshape(kind_count, box, proj_count, box, box)
     table = jnp.transpose(table, (0, 1, 3, 2, 4)).reshape(kind_count, box, box, lanes)
     table = jnp.pad(table, ((0, 0), (0, 1), (0, 0), (0, 0)))
@@ -318,7 +330,9 @@
         name="project",
     )(wave, table, coupling, kinds, centres, species)
     reach = (box + planes - 2) // planes
-    coef = coef + sum(passed_along(coef, step) for hop in range(reach) for step in (hop + 1, -hop - 1))
+    coef = coef + sum(
+        passed_along(coef, "grid", step) for hop in range(reach) for step in (hop + 1, -hop - 1)
+    )
     local = pl.pallas_call(
         local_kernel,
         out_shape=shape((rows * planes, extent + box, extent)),
@@ -352,16 +366,15 @@
         cost_estimate=cost(40 * wave.size, 20 * size),
         name="spread",
     )(local, table, coef, centres, species)
-    update = pl.pallas_call(
+    return pl.pallas_call(
         finish_kernel,
-        out_shape=shape(wave.shape),
-        in_specs=[VMEM, VMEM],
-        out_specs=VMEM,
+        out_shape=(shape(wave.shape), density_shape),
+        in_specs=[VMEM] * (2 + shares),
+        out_specs=(VMEM, VMEM),
         compiler_params=params(),
         cost_estimate=cost(4 * wave.size, 3 * size),
         name="finish",
-    )(local, back)
-    return (update, density)
+    )(local, back, *terms)
 
 
 def solution(mesh):

time: 82.2 us -> 70.2 us (0.85)
  between operations: 14.8 us -> 1.41 us
  Pallas kernels: 26.5 us -> 19.9 us
  waiting for transfers between devices: 14.5 us -> 19 us
  local copies, waits for them, and re-layouts: 9.33 us -> 11.7 us
  starting transfers between devices: 16.6 us -> 17.8 us
    pallas_call x1, Pallas kernels: 14.4 us -> 9.57 us  [per_device(): pl.pallas_call(spread_kernel, out_shape=shape(local.shape), in_specs=[VME...]
    all_to_all x1, waiting for transfers between devices: 9.09 us -> 12.4 us  [per_device(): back = lax.all_to_all(along, 'grid', 0, 0, tiled=True)]
    unnamed x16 -> x22, local copies, waits for them, and re-layouts: 1.25 us -> 3.6 us
    ppermute x4 -> x5, waiting for transfers between devices: 4.75 us -> 6.57 us  [passed_along(): return lax.ppermute(value, axis, pairs)]
    pallas_call x1, Pallas kernels: 6.94 us -> 5.16 us  [per_device(): pl.pallas_call(project_kernel, out_shape=shape((rows, proj_count, atom_co...]
    ppermute x4 -> x5, starting transfers between devices: 5.59 us -> 7.11 us  [passed_along(): return lax.ppermute(value, axis, pairs)]
  transfers between devices with their start and end apart: 7 -> 7, of which waited for: 3 -> 3; matrix products, arithmetic and copies ran while one was open for 10% -> 12% of each run, Pallas kernels for 29% -> 23%
where the time goes in v2:
time: 70.2 us; the launch traced here: 69.7 us
  Pallas kernels  19.9 us (28%)
  waiting for transfers between devices  19 us (27%)
  starting transfers between devices  17.8 us (25%)
  local copies, waits for them, and re-layouts  11.7 us (17%)
  between operations  1.41 us (2%)
    all_to_all x1, waiting for transfers between devices, per_device(): back = lax.all_to_all(along, 'grid', 0, 0, tiled=True)  12.4 us
    pallas_call x1, Pallas kernels, per_device(): pl.pallas_call(spread_kernel, out_shape=shape(local.shape), in_specs=[VME...  9.57 us
    ppermute x5, starting transfers between devices, passed_along(): return lax.ppermute(value, axis, pairs)  7.11 us
    ppermute x5, waiting for transfers between devices, passed_along(): return lax.ppermute(value, axis, pairs)  6.57 us
    all_to_all x1, starting transfers between devices, per_device(): held = lax.all_to_all(send, 'grid', 0, 0, tiled=True)  6.16 us
    pallas_call x1, Pallas kernels, per_device(): pl.pallas_call(project_kernel, out_shape=shape((rows, proj_count, atom_co...  5.16 us
    all_to_all x1, starting transfers between devices, per_device(): back = lax.all_to_all(along, 'grid', 0, 0, tiled=True)  4.57 us
    transpose x1, local copies, waits for them, and re-layouts, per_device(): jnp.transpose(table, (0, 1, 3, 2, 4)).reshape(kind_count, box, box, lanes)  3.78 us
  transfers between devices with their start and end apart: 7, of which 3 were waited for; matrix products, arithmetic and copies ran while one was open for 12% of the time, Pallas kernels for 23%

profile of v2, /device:TPU:16, one launch (start us, length us, event | category | flops | bytes accessed | tf_op | source)
XLA Modules:
  0.0 69.7 jit_solution(10371627263639932332)
XLA Ops:
  1.3 0.0 copy-start
  1.3 1.2 %copy-done = f32[2,1,8,128,128]{4,3,2,1,0:T(8,128)S(1)} copy-done((f32[2,1,8,128,128]{4,3,2,1,0:T(8,128)S(1)}, f32[2,1,8,128,128]{4,3,2,1,0:T(8,128)}, u32[]{:S(2)}) %copy-start) | copy-done | bytes 1048600
  2.5 0.0 copy-start.10
  2.5 1.3 %pack.1 = (f32[16,2,64,128]{3,2,1,0:T(8,128)}, f32[8,64,128]{2,1,0:T(8,128)S(1)}, f32[8,64,128]{2,1,0:T(8,128)S(1)}) custom-call(f32[2,1,8,128,128]{4,3,2,1,0:T(8,128)S(1)} %copy-done, f32[1]{0:T(128)S(6)} %copy.11.occ_ref), custom_call_target="tpu_custom_call" | custom-call | flops 262144 | bytes 2097152 | tf_op jit(solution)/shard_map/pack/pallas_call | solution.py:303
  3.8 0.0 copy-start.9
  3.8 0.7 %copy-done.9 = f32[8,64,128]{2,1,0:T(8,128)} copy-done((f32[8,64,128]{2,1,0:T(8,128)}, f32[8,64,128]{2,1,0:T(8,128)S(1)}, u32[]{:S(2)}) %copy-start.9) | copy-done | bytes 262168
  4.5 6.2 %all-to-all-start = ((f32[16,2,64,128]{3,2,1,0:T(8,128)}), f32[16,2,64,128]{3,2,1,0:T(8,128)S(1)}, u32[]{:S(2)}, u32[]{:S(2)}) async-start(f32[16,2,64,128]{3,2,1,0:T(8,128)} %get-tuple-element.5), calls=%async_computation | async-start | bytes 2097152 | tf_op jit(solution)/shard_map/all_to_all | solution.py:312
  10.7 0.0 copy-done.10
  10.7 2.0 %reshape.16 = f32[2,16,8,16,16]{4,3,2,1,0:T(8,128)} reshape(f32[2,16,8,256]{3,2,1,0:T(8,128)S(1)} %copy-done.10) | data formatting | bytes 524288 | tf_op jit(solution)/shard_map/reshape | solution.py:314
  12.7 3.8 %copy.10 = f32[2,16,16,8,16]{4,3,2,1,0:T(8,128)} copy(f32[2,16,16,8,16]{4,2,3,1,0:T(8,128)} %bitcast.10) | data formatting | bytes 524288 | tf_op jit(solution)/shard_map/transpose | solution.py:315
  16.4 0.0 copy-start.1
  16.4 0.0 copy-start.6
  16.4 0.0 copy-start.7
  16.4 0.0 copy-start.8
  16.4 0.0 copy-start.3
  16.5 2.3 %reshape.17 = f32[2,16,16,128]{3,2,1,0:T(8,128)S(1)} reshape(f32[2,16,16,8,16]{4,3,2,1,0:T(8,128)} %copy.10) | data formatting | bytes 524288 | tf_op jit(solution)/shard_map/reshape | solution.py:315
  18.8 0.0 copy-done.1
  18.8 0.0 copy-done.6
  18.8 0.0 copy-done.7
  18.8 0.0 copy-done.8
  18.8 5.2 %project.1 = f32[2,8,128]{2,1,0:T(8,128)S(1)} custom-call(f32[2,1,8,128,128]{4,3,2,1,0:T(8,128)S(1)} %copy-done.1, f32[34,16,128]{2,1,0:T(8,128)S(1)} %bitcast.7, f32[2,8,8]{2,1,0:T(8,128)S(1)} %copy-done.6, s32[1,128]{1,0:T(1,128)S(1)} %bitcast.9, s32[3,128]{1,0:T(4,128)S(1)} %copy-done.7, s32[128]{0:T(128)S(1)} %copy-done.8), custom_call_target="tpu_custom_call" | custom-call | flops 10485760 | bytes 20971520 | tf_op jit(solution)/shard_map/project/pallas_call | solution.py:318
  24.0 0.4 collective-permute-start
  24.4 2.3 %collective-permute-start.1 = (f32[2,8,128]{2,1,0:T(8,128)S(1)}, f32[2,8,128]{2,1,0:T(8,128)S(1)}, u32[]{:S(2)}, u32[]{:S(2)}) collective-permute-start(f32[2,8,128]{2,1,0:T(8,128)S(1)} %project.1), channel_id=1, source_target_pairs={{0,30},{2,0},{4,2},{6,4},{8,6},{10,8},{12,10},{14,12},{16,14},{18,... | collective-permute-start | bytes 24584 | tf_op jit(solution)/shard_map/ppermute | solution.py:21
  26.6 0.4 collective-permute-start.2
  27.1 2.5 %collective-permute-start.3 = (f32[2,8,128]{2,1,0:T(8,128)S(1)}, f32[2,8,128]{2,1,0:T(8,128)S(1)}, u32[]{:S(2)}, u32[]{:S(2)}) collective-permute-start(f32[2,8,128]{2,1,0:T(8,128)S(1)} %project.1), channel_id=1, source_target_pairs={{0,28},{2,30},{4,0},{6,2},{8,4},{10,6},{12,8},{14,10},{16,12},{18,... | collective-permute-start | bytes 24584 | tf_op jit(solution)/shard_map/ppermute | solution.py:21
  29.5 6.0 %collective-permute-done = f32[2,8,128]{2,1,0:T(8,128)S(1)} collective-permute-done((f32[2,8,128]{2,1,0:T(8,128)S(1)}, f32[2,8,128]{2,1,0:T(8,128)S(1)}, u32[]{:S(2)}, u32[]{:S(2)}) %collective-permute-start) | collective-permute-done | bytes 8224 | tf_op jit(solution)/shard_map/ppermute | solution.py:21
  35.5 0.0 collective-permute-done.1
  35.6 0.6 collective-permute-done.2
  36.1 0.0 collective-permute-done.3
  36.1 0.0 copy-start.2
  36.1 0.0 all-to-all-done.held_ref
  36.1 0.0 copy-done.3
  36.2 1.5 %along_x.1 = f32[16,2,64,128]{3,2,1,0:T(8,128)} custom-call(f32[16,2,64,128]{3,2,1,0:T(8,128)S(1)} %all-to-all-done.held_ref, bf16[2,128,128]{2,1,0:T(8,128)(2,1)S(1)} %copy-done.3, f32[2,8,128]{2,1,0:T(8,128)S(1)} %add_add_fusion.coef_ref), custom_call_target="tpu_custom_call" | custom-call | flops 201326592 | bytes 2097152 | tf_op jit(solution)/shard_map/along_x/pallas_call | solution.py:345
  37.7 4.6 %all-to-all-start.1 = ((f32[16,2,64,128]{3,2,1,0:T(8,128)}), f32[16,2,64,128]{3,2,1,0:T(8,128)S(1)}, u32[]{:S(2)}, u32[]{:S(2)}) async-start(f32[16,2,64,128]{3,2,1,0:T(8,128)} %along_x.1), calls=%async_computation.1 | async-start | bytes 2097152 | tf_op jit(solution)/shard_map/all_to_all | solution.py:355
  42.3 1.5 %collective-permute-start.4 = (f32[8,64,128]{2,1,0:T(8,128)}, f32[8,64,128]{2,1,0:T(8,128)S(1)}, u32[]{:S(2)}, u32[]{:S(2)}) collective-permute-start(f32[8,64,128]{2,1,0:T(8,128)} %copy-done.9), channel_id=1, source_target_pairs={{0,1},{1,0},{2,3},{3,2},{4,5},{5,4},{6,7},{7,6},{8,9},{9,8},{10,11... | collective-permute-start | bytes 786440 | tf_op jit(solution)/shard_map/ppermute | solution.py:21
  43.8 0.0 copy-done.2
  43.8 1.0 %local.1.local_ref = f32[16,144,128]{2,1,0:T(8,128)S(1)} custom-call(f32[2,1,8,128,128]{4,3,2,1,0:T(8,128)S(1)} %copy-done.1, f32[8,128,128]{2,1,0:T(8,128)S(1)} %copy-done.2, bf16[2,128,128]{2,1,0:T(8,128)(2,1)S(1)} %copy-done.3), custom_call_target="tpu_custom_call" | custom-call | flops 402653184 | bytes 3145728 | tf_op jit(solution)/shard_map/local/pallas_call | solution.py:336
  44.8 9.6 %spread.1.local_ref = f32[16,144,128]{2,1,0:T(8,128)S(1)} custom-call(f32[16,144,128]{2,1,0:T(8,128)S(1)} %local.1.local_ref, f32[34,16,128]{2,1,0:T(8,128)S(1)} %bitcast.8, f32[2,8,128]{2,1,0:T(8,128)S(1)} %add_add_fusion.coef_ref, s32[3,128]{1,0:T(4,128)S(1)} %copy-done.7, s32[128]{0:T(128)S(1)} %copy-done.8), custom_call_target="tpu_custom_call" | custom-call | flops 10485760 | bytes 20971520 | tf_op jit(solution)/shard_map/spread/pallas_call | solution.py:356
  54.4 0.0 collective-permute-done.4.refs_1_
  54.4 0.0 copy-start.4
  54.4 0.7 copy-done.4
  55.1 12.4 %all-to-all-done.1.along_ref = f32[16,2,64,128]{3,2,1,0:T(8,128)S(1)} async-done(((f32[16,2,64,128]{3,2,1,0:T(8,128)}), f32[16,2,64,128]{3,2,1,0:T(8,128)S(1)}, u32[]{:S(2)}, u32[]{:S(2)}) %all-to-all-start.1) | async-done | bytes 1048608 | tf_op jit(solution)/shard_map/all_to_all | solution.py:355
  67.5 0.0 copy-start.5
  67.5 0.9 %copy-done.5 = f32[8,64,128]{2,1,0:T(8,128)S(1)} copy-done((f32[8,64,128]{2,1,0:T(8,128)S(1)}, f32[8,64,128]{2,1,0:T(8,128)}, u32[]{:S(2)}) %copy-start.5) | copy-done | bytes 262168
  68.4 1.3 %finish.1 = (f32[2,1,8,128,128]{4,3,2,1,0:T(8,128)}, f32[8,64,128]{2,1,0:T(8,128)}) custom-call(f32[16,144,128]{2,1,0:T(8,128)S(1)} %spread.1.local_ref, f32[16,2,64,128]{3,2,1,0:T(8,128)S(1)} %all-to-all-done.1.along_ref, f32[8,64,128]{2,1,0:T(8,128)S(1)} %get-tuple-element.6.refs_0_, f32[8,64,128]{2,1,0:T(8,128)S(1)} %copy-done.5), custom_call_target="tpu_custom_call" | custom-call | flops 1048576 | bytes 3145728 | tf_op jit(solution)/shard_map/finish/pallas_call | solution.py:369
  (2 shorter events, 0.0 us)
Async XLA Ops:
  1.3 1.2 %copy-start = (f32[2,1,8,128,128]{4,3,2,1,0:T(8,128)S(1)}, f32[2,1,8,128,128]{4,3,2,1,0:T(8,128)}, u32[]{:S(2)}) copy-start(f32[2,1,8,128,128]{4,3,2,1,0:T(8,128)} %wave_ref.5) | copy-start | bytes 3145732
  2.5 8.2 %copy-start.10 = (f32[2,16,8,256]{3,2,1,0:T(8,128)S(1)}, f32[2,16,8,256]{3,2,1,0:T(8,128)}, u32[]{:S(2)}) copy-start(f32[2,16,8,256]{3,2,1,0:T(8,128)} %param.13) | copy-start | bytes 786436
  3.8 0.7 %copy-start.9 = (f32[8,64,128]{2,1,0:T(8,128)}, f32[8,64,128]{2,1,0:T(8,128)S(1)}, u32[]{:S(2)}) copy-start(f32[8,64,128]{2,1,0:T(8,128)S(1)} %get-tuple-element.7) | copy-start | bytes 786436
  4.5 31.6 %all-to-all-start = ((f32[16,2,64,128]{3,2,1,0:T(8,128)}), f32[16,2,64,128]{3,2,1,0:T(8,128)S(1)}, u32[]{:S(2)}, u32[]{:S(2)}) async-start(f32[16,2,64,128]{3,2,1,0:T(8,128)} %get-tuple-element.5), calls=%async_computation | async-start | bytes 2097152 | tf_op jit(solution)/shard_map/all_to_all | solution.py:312
  16.4 2.3 %copy-start.1 = (f32[2,1,8,128,128]{4,3,2,1,0:T(8,128)S(1)}, f32[2,1,8,128,128]{4,3,2,1,0:T(8,128)}, u32[]{:S(2)}) copy-start(f32[2,1,8,128,128]{4,3,2,1,0:T(8,128)} %wave_ref.5) | copy-start | bytes 3145732
  16.4 2.3 %copy-start.6 = (f32[2,8,8]{2,1,0:T(8,128)S(1)}, f32[2,8,8]{2,1,0:T(8,128)}, u32[]{:S(2)}) copy-start(f32[2,8,8]{2,1,0:T(8,128)} %coupling_ref.1) | copy-start | bytes 1540
  16.4 2.3 %copy-start.7 = (s32[3,128]{1,0:T(4,128)S(1)}, s32[3,128]{1,0:T(4,128)}, u32[]{:S(2)}) copy-start(s32[3,128]{1,0:T(4,128)} %centres_ref.3) | copy-start | bytes 4612
  16.4 2.3 %copy-start.8 = (s32[128]{0:T(128)S(1)}, s32[128]{0:T(128)}, u32[]{:S(2)}) copy-start(s32[128]{0:T(128)} %species_ref.3) | copy-start | bytes 1540
  16.4 19.7 %copy-start.3 = (bf16[2,128,128]{2,1,0:T(8,128)(2,1)S(1)}, bf16[2,128,128]{2,1,0:T(8,128)(2,1)}, u32[]{:S(2)}) copy-start(bf16[2,128,128]{2,1,0:T(8,128)(2,1)} %constant.5.clone.matrix_ref) | copy-start | bytes 196612
  24.0 11.6 %collective-permute-start = (f32[2,8,128]{2,1,0:T(8,128)S(1)}, f32[2,8,128]{2,1,0:T(8,128)S(1)}, u32[]{:S(2)}, u32[]{:S(2)}) collective-permute-start(f32[2,8,128]{2,1,0:T(8,128)S(1)} %project.1), channel_id=1, source_target_pairs={{0,2},{2,4},{4,6},{6,8},{8,10},{10,12},{12,14},{14,16},{16,18},{18... | collective-permute-start | bytes 24584 | tf_op jit(solution)/shard_map/ppermute | solution.py:21
  24.4 11.2 %collective-permute-start.1 = (f32[2,8,128]{2,1,0:T(8,128)S(1)}, f32[2,8,128]{2,1,0:T(8,128)S(1)}, u32[]{:S(2)}, u32[]{:S(2)}) collective-permute-start(f32[2,8,128]{2,1,0:T(8,128)S(1)} %project.1), channel_id=1, source_target_pairs={{0,30},{2,0},{4,2},{6,4},{8,6},{10,8},{12,10},{14,12},{16,14},{18,... | collective-permute-start | bytes 24584 | tf_op jit(solution)/shard_map/ppermute | solution.py:21
  26.6 9.5 %collective-permute-start.2 = (f32[2,8,128]{2,1,0:T(8,128)S(1)}, f32[2,8,128]{2,1,0:T(8,128)S(1)}, u32[]{:S(2)}, u32[]{:S(2)}) collective-permute-start(f32[2,8,128]{2,1,0:T(8,128)S(1)} %project.1), channel_id=1, source_target_pairs={{0,4},{2,6},{4,8},{6,10},{8,12},{10,14},{12,16},{14,18},{16,20},{1... | collective-permute-start | bytes 24584 | tf_op jit(solution)/shard_map/ppermute | solution.py:21
  27.1 9.0 %collective-permute-start.3 = (f32[2,8,128]{2,1,0:T(8,128)S(1)}, f32[2,8,128]{2,1,0:T(8,128)S(1)}, u32[]{:S(2)}, u32[]{:S(2)}) collective-permute-start(f32[2,8,128]{2,1,0:T(8,128)S(1)} %project.1), channel_id=1, source_target_pairs={{0,28},{2,30},{4,0},{6,2},{8,4},{10,6},{12,8},{14,10},{16,12},{18,... | collective-permute-start | bytes 24584 | tf_op jit(solution)/shard_map/ppermute | solution.py:21
  36.1 7.7 %copy-start.2 = (f32[8,128,128]{2,1,0:T(8,128)S(1)}, f32[8,128,128]{2,1,0:T(8,128)}, u32[]{:S(2)}) copy-start(f32[8,128,128]{2,1,0:T(8,128)} %potential_ref.1) | copy-start | bytes 1572868
  37.7 29.7 %all-to-all-start.1 = ((f32[16,2,64,128]{3,2,1,0:T(8,128)}), f32[16,2,64,128]{3,2,1,0:T(8,128)S(1)}, u32[]{:S(2)}, u32[]{:S(2)}) async-start(f32[16,2,64,128]{3,2,1,0:T(8,128)} %along_x.1), calls=%async_computation.1 | async-start | bytes 2097152 | tf_op jit(solution)/shard_map/all_to_all | solution.py:355
  42.3 12.1 %collective-permute-start.4 = (f32[8,64,128]{2,1,0:T(8,128)}, f32[8,64,128]{2,1,0:T(8,128)S(1)}, u32[]{:S(2)}, u32[]{:S(2)}) collective-permute-start(f32[8,64,128]{2,1,0:T(8,128)} %copy-done.9), channel_id=1, source_target_pairs={{0,1},{1,0},{2,3},{3,2},{4,5},{5,4},{6,7},{7,6},{8,9},{9,8},{10,11... | collective-permute-start | bytes 786440 | tf_op jit(solution)/shard_map/ppermute | solution.py:21
  54.4 0.7 %copy-start.4 = (f32[8,64,128]{2,1,0:T(8,128)}, f32[8,64,128]{2,1,0:T(8,128)S(1)}, u32[]{:S(2)}) copy-start(f32[8,64,128]{2,1,0:T(8,128)S(1)} %collective-permute-done.4.refs_1_) | copy-start | bytes 786436
  67.5 1.0 %copy-start.5 = (f32[8,64,128]{2,1,0:T(8,128)S(1)}, f32[8,64,128]{2,1,0:T(8,128)}, u32[]{:S(2)}) copy-start(f32[8,64,128]{2,1,0:T(8,128)} %copy-done.4) | copy-start | bytes 786436

commit v3 on v1

--- a/solution.py
+++ b/solution.py
@@ -15,10 +15,10 @@
 SMEM = pl.BlockSpec(memory_space=pltpu.SMEM)
 
 
-def passed_along(value, steps):
-    count = lax.axis_size("grid")
+def passed_along(value, axis, steps):
+    count = lax.axis_size(axis)
     pairs = [(source, (source + steps) % count) for source in range(count)]
-    return lax.ppermute(value, "grid", pairs)
+    return lax.ppermute(value, axis, pairs)
 
 
 def params():
@@ -50,18 +50,11 @@
     return dot(left[0], right[0]) + (dot(left[0], right[1]) + dot(left[1], right[0]))
 
 
-def pack_kernel(wave_ref, occ_ref, send_ref, density_ref):
+def pack_kernel(wave_ref, send_ref):
     _, orbitals, planes, extent, _ = wave_ref.shape
     count = send_ref.shape[0]
     width = extent // count
     for p in range(planes):
-        total = None
-        for o in range(orbitals):
-            real = wave_ref[0, o, p]
-            imag = wave_ref[1, o, p]
-            term = occ_ref[o] * (real * real + imag * imag)
-            total = term if total is None else total + term
-        density_ref[p] = total
         for c in range(2):
             for o in range(orbitals):
                 for d in range(count):
@@ -185,8 +178,21 @@
         coef_ref[r] = scaled
 
 
-def local_kernel(wave_ref, potential_ref, matrix_ref, out_ref):
+def local_kernel(wave_ref, potential_ref, matrix_ref, occ_ref, out_ref, *density_refs):
     _, orbitals, planes, extent, _ = wave_ref.shape
+    shares = len(density_refs)
+    share = extent // shares
+    place = lax.axis_index("orb")
+    for p in range(planes):
+        for k in range(shares):
+            taken = pl.ds(pl.multiple_of(lax.rem(place + k, shares) * share, share), share)
+            total = None
+            for o in range(orbitals):
+                real = wave_ref[0, o, p, taken, :]
+                imag = wave_ref[1, o, p, taken, :]
+                term = occ_ref[o] * (real * real + imag * imag)
+                total = term if total is None else total + term
+            density_refs[k][p] = total
     box = out_ref.shape[1] - extent
     matrix = (matrix_ref[0], matrix_ref[1])
     for c in range(2):
@@ -288,17 +294,18 @@
     size = wave.size * 4
     matrix = second_derivative(extent)
     kinds = species.reshape(1, atom_count)
-    send, density_term = pl.pallas_call(
+    shares = lax.axis_size("orb")
+    density_shape = shape((planes, extent // shares, extent))
+    send = pl.pallas_call(
         pack_kernel,
-        out_shape=(shape((count, rows, width * planes, extent)), shape((planes, extent, extent))),
-        in_specs=[VMEM, SMEM],
-        out_specs=(VMEM, VMEM),
+        out_shape=shape((count, rows, width * planes, extent)),
+        in_specs=[VMEM],
+        out_specs=VMEM,
         compiler_params=params(),
         cost_estimate=cost(wave.size, 2 * size),
         name="pack",
-    )(wave, occupations)
+    )(wave)
     held = lax.all_to_all(send, "grid", 0, 0, tiled=True)
-    density = lax.psum_scatter(density_term, "orb", scatter_dimension=1, tiled=True)
     table = projectors.reshape(kind_count, box, proj_count, box, box)
     table = jnp.transpose(table, (0, 1, 3, 2, 4)).reshape(kind_count, box, box, lanes)
     table = jnp.pad(table, ((0, 0), (0, 1), (0, 0), (0, 0)))
@@ -318,16 +325,22 @@
         name="project",
     )(wave, table, coupling, kinds, centres, species)
     reach = (box + planes - 2) // planes
-    coef = coef + sum(passed_along(coef, step) for hop in range(reach) for step in (hop + 1, -hop - 1))
-    local = pl.pallas_call(
+    own_coef = coef
+    coef = coef + sum(
+        passed_along(coef, "grid", step) for hop in range(reach) for step in (hop + 1, -hop - 1)
+    )
+    local, *terms = pl.pallas_call(
         local_kernel,
-        out_shape=shape((rows * planes, extent + box, extent)),
-        in_specs=[VMEM] * 3,
-        out_specs=VMEM,
+        out_shape=[shape((rows * planes, extent + box, extent))] + [density_shape] * shares,
+        in_specs=[VMEM] * 3 + [SMEM],
+        out_specs=[VMEM] * (shares + 1),
         compiler_params=params(),
         cost_estimate=cost(12 * extent * wave.size, 3 * size),
         name="local",
-    )(wave, potential, matrix)
+    )(wave, potential, matrix, occupations)
+    density = terms[0]
+    for k in range(1, shares):
+        density = density + passed_along(terms[k], "orb", k)
     along = pl.pallas_call(
         along_x_kernel,
         out_shape=shape(held.shape),
@@ -337,7 +350,7 @@
         compiler_params=params(),
         cost_estimate=cost(6 * extent * wave.size, 2 * size),
         name="along_x",
-    )(held, matrix, coef)
+    )(held, matrix, own_coef)
     back = lax.all_to_all(along, "grid", 0, 0, tiled=True)
     local = pl.pallas_call(
         spread_kernel,

time: 82.2 us -> 79.1 us (0.962)
  waiting for transfers between devices: 14.5 us -> 31 us
  between operations: 14.8 us -> 1.4 us
  Pallas kernels: 26.5 us -> 21.1 us
  local copies, waits for them, and re-layouts: 9.33 us -> 6.39 us
  starting transfers between devices: 16.6 us -> 17.9 us
    all_to_all x1, waiting for transfers between devices: 0.01 us -> 14.4 us  [per_device(): held = lax.all_to_all(send, 'grid', 0, 0, tiled=True)]
    ppermute x4 -> x5, waiting for transfers between devices: 4.75 us -> 16.6 us  [passed_along(): return lax.ppermute(value, axis, pairs)]
    all_to_all x1, waiting for transfers between devices: 9.09 us -> 0.01 us  [per_device(): back = lax.all_to_all(along, 'grid', 0, 0, tiled=True)]
    pallas_call x1, Pallas kernels: 14.4 us -> 10.5 us  [per_device(): pl.pallas_call(spread_kernel, out_shape=shape(local.shape), in_specs=[VME...]
    transpose x1, local copies, waits for them, and re-layouts: 3.79 us -> 2.22 us  [per_device(): jnp.transpose(table, (0, 1, 3, 2, 4)).reshape(kind_count, box, box, lanes)]
    ppermute x4 -> x5, starting transfers between devices: 5.59 us -> 7.14 us  [passed_along(): return lax.ppermute(value, axis, pairs)]
    pallas_call x1, Pallas kernels: 6.94 us -> 5.52 us  [per_device(): pl.pallas_call(project_kernel, out_shape=shape((rows, proj_count, atom_co...]
    reshape x1, local copies, waits for them, and re-layouts: 2 us -> 0.63 us  [per_device(): table = projectors.reshape(kind_count, box, proj_count, box, box)]
  transfers between devices with their start and end apart: 7 -> 7, of which waited for: 3 -> 3; matrix products, arithmetic and copies ran while one was open for 10% -> 7% of each run, Pallas kernels for 29% -> 22%
where the time goes in v3:
time: 79.1 us; the launch traced here: 78.6 us
  waiting for transfers between devices  31 us (39%)
  Pallas kernels  21.1 us (27%)
  starting transfers between devices  17.9 us (23%)
  local copies, waits for them, and re-layouts  6.39 us (8%)
  between operations  1.4 us (2%)
    ppermute x5, waiting for transfers between devices, passed_along(): return lax.ppermute(value, axis, pairs)  16.6 us
    all_to_all x1, waiting for transfers between devices, per_device(): held = lax.all_to_all(send, 'grid', 0, 0, tiled=True)  14.4 us
    pallas_call x1, Pallas kernels, per_device(): pl.pallas_call(spread_kernel, out_shape=shape(local.shape), in_specs=[VME...  10.5 us
    ppermute x5, starting transfers between devices, passed_along(): return lax.ppermute(value, axis, pairs)  7.14 us
    all_to_all x1, starting transfers between devices, per_device(): held = lax.all_to_all(send, 'grid', 0, 0, tiled=True)  6.16 us
    pallas_call x1, Pallas kernels, per_device(): pl.pallas_call(project_kernel, out_shape=shape((rows, proj_count, atom_co...  5.52 us
    all_to_all x1, starting transfers between devices, per_device(): back = lax.all_to_all(along, 'grid', 0, 0, tiled=True)  4.64 us
    reshape x1, local copies, waits for them, and re-layouts, per_device(): jnp.transpose(table, (0, 1, 3, 2, 4)).reshape(kind_count, box, box, lanes)  2.26 us
  transfers between devices with their start and end apart: 7, of which 3 were waited for; matrix products, arithmetic and copies ran while one was open for 7% of the time, Pallas kernels for 22%

profile of v3, /device:TPU:16, one launch (start us, length us, event | category | flops | bytes accessed | tf_op | source)
XLA Modules:
  0.0 78.6 jit_solution(7428400369890360222)
XLA Ops:
  0.6 0.0 copy-start
  0.6 1.2 %copy-done = f32[2,1,8,128,128]{4,3,2,1,0:T(8,128)S(1)} copy-done((f32[2,1,8,128,128]{4,3,2,1,0:T(8,128)S(1)}, f32[2,1,8,128,128]{4,3,2,1,0:T(8,128)}, u32[]{:S(2)}) %copy-start) | copy-done | bytes 1048600
  1.9 0.0 copy-start.7
  1.9 1.2 %pack.1 = f32[16,2,64,128]{3,2,1,0:T(8,128)} custom-call(f32[2,1,8,128,128]{4,3,2,1,0:T(8,128)S(1)} %copy-done), custom_call_target="tpu_custom_call" | custom-call | flops 262144 | bytes 2097152 | tf_op jit(solution)/shard_map/pack/pallas_call | solution.py:299
  3.1 6.2 %all-to-all-start = ((f32[16,2,64,128]{3,2,1,0:T(8,128)}), f32[16,2,64,128]{3,2,1,0:T(8,128)S(1)}, u32[]{:S(2)}, u32[]{:S(2)}) async-start(f32[16,2,64,128]{3,2,1,0:T(8,128)} %pack.1), calls=%async_computation | async-start | bytes 2097152 | tf_op jit(solution)/shard_map/all_to_all | solution.py:308
  9.3 0.0 copy-done.7
  9.3 0.6 reshape.16
  9.9 2.2 %copy.10 = f32[2,16,16,8,16]{4,3,2,1,0:T(8,128)} copy(f32[2,16,16,8,16]{4,2,3,1,0:T(8,128)S(1)} %bitcast.10) | data formatting | bytes 524288 | tf_op jit(solution)/shard_map/transpose | solution.py:310
  12.1 0.0 copy-start.1
  12.1 0.0 copy-start.4
  12.1 0.0 copy-start.5
  12.1 0.0 copy-start.6
  12.1 0.0 copy-start.3
  12.2 2.3 %reshape.17 = f32[2,16,16,128]{3,2,1,0:T(8,128)S(1)} reshape(f32[2,16,16,8,16]{4,3,2,1,0:T(8,128)} %copy.10) | data formatting | bytes 524288 | tf_op jit(solution)/shard_map/reshape | solution.py:310
  14.5 0.0 copy-done.1
  14.5 0.0 copy-done.4
  14.5 0.0 copy-done.5
  14.5 0.0 copy-done.6
  14.5 5.5 %project.1.coef_ref = f32[2,8,128]{2,1,0:T(8,128)S(1)} custom-call(f32[2,1,8,128,128]{4,3,2,1,0:T(8,128)S(1)} %copy-done.1, f32[34,16,128]{2,1,0:T(8,128)S(1)} %bitcast.7, f32[2,8,8]{2,1,0:T(8,128)S(1)} %copy-done.4, s32[1,128]{1,0:T(1,128)S(1)} %bitcast.9, s32[3,128]{1,0:T(4,128)S(1)} %copy-done.5, s32[128]{0:T(128)S(1)} %copy-done.6), custom_call_target="tpu_custom_call" | custom-call | flops 10485760 | bytes 20971520 | tf_op jit(solution)/shard_map/project/pallas_call | solution.py:313
  20.0 0.0 copy-start.2
  20.0 14.4 %all-to-all-done.held_ref = f32[16,2,64,128]{3,2,1,0:T(8,128)S(1)} async-done(((f32[16,2,64,128]{3,2,1,0:T(8,128)}), f32[16,2,64,128]{3,2,1,0:T(8,128)S(1)}, u32[]{:S(2)}, u32[]{:S(2)}) %all-to-all-start) | async-done | bytes 1048608 | tf_op jit(solution)/shard_map/all_to_all | solution.py:308
  34.4 0.0 copy-done.3
  34.4 1.5 %along_x.1 = f32[16,2,64,128]{3,2,1,0:T(8,128)} custom-call(f32[16,2,64,128]{3,2,1,0:T(8,128)S(1)} %all-to-all-done.held_ref, bf16[2,128,128]{2,1,0:T(8,128)(2,1)S(1)} %copy-done.3, f32[2,8,128]{2,1,0:T(8,128)S(1)} %project.1.coef_ref), custom_call_target="tpu_custom_call" | custom-call | flops 201326592 | bytes 2097152 | tf_op jit(solution)/shard_map/along_x/pallas_call | solution.py:344
  36.0 4.6 %all-to-all-start.1 = ((f32[16,2,64,128]{3,2,1,0:T(8,128)}), f32[16,2,64,128]{3,2,1,0:T(8,128)S(1)}, u32[]{:S(2)}, u32[]{:S(2)}) async-start(f32[16,2,64,128]{3,2,1,0:T(8,128)} %along_x.1), calls=%async_computation.1 | async-start | bytes 2097152 | tf_op jit(solution)/shard_map/all_to_all | solution.py:354
  41.3 0.0 copy-done.2
  41.3 1.1 %local.1 = (f32[16,144,128]{2,1,0:T(8,128)S(1)}, f32[8,64,128]{2,1,0:T(8,128)S(1)}, f32[8,64,128]{2,1,0:T(8,128)S(1)}) custom-call(f32[2,1,8,128,128]{4,3,2,1,0:T(8,128)S(1)} %copy-done.1, f32[8,128,128]{2,1,0:T(8,128)S(1)} %copy-done.2, bf16[2,128,128]{2,1,0:T(8,128)(2,1)S(1)} %copy-done.3, f32[1]{0:T(128)S(6)} %copy.11.occ_ref), custom_call_target="tpu_custom_call" | custom-call | flops 402653184 | bytes 3145728 | tf_op jit(solution)/shard_map/local/pallas_call | solution.py:332
  42.3 1.6 %collective-permute-start.4 = (f32[8,64,128]{2,1,0:T(8,128)S(1)}, f32[8,64,128]{2,1,0:T(8,128)S(1)}, u32[]{:S(2)}, u32[]{:S(2)}) collective-permute-start(f32[8,64,128]{2,1,0:T(8,128)S(1)} %get-tuple-element.7), channel_id=1, source_target_pairs={{0,1},{1,0},{2,3},{3,2},{4,5},{5,4},{6,7},{7,6},{8,9},{9,8},{10,11... | collective-permute-start | bytes 786440 | tf_op jit(solution)/shard_map/ppermute | solution.py:21
  43.9 0.0 collective-permute-start
  43.9 2.6 %collective-permute-start.1 = (f32[2,8,128]{2,1,0:T(8,128)S(1)}, f32[2,8,128]{2,1,0:T(8,128)S(1)}, u32[]{:S(2)}, u32[]{:S(2)}) collective-permute-start(f32[2,8,128]{2,1,0:T(8,128)S(1)} %project.1.coef_ref), channel_id=1, source_target_pairs={{0,30},{2,0},{4,2},{6,4},{8,6},{10,8},{12,10},{14,12},{16,14},{18,... | collective-permute-start | bytes 24584 | tf_op jit(solution)/shard_map/ppermute | solution.py:21
  46.6 0.6 collective-permute-start.2
  47.1 2.4 %collective-permute-start.3 = (f32[2,8,128]{2,1,0:T(8,128)S(1)}, f32[2,8,128]{2,1,0:T(8,128)S(1)}, u32[]{:S(2)}, u32[]{:S(2)}) collective-permute-start(f32[2,8,128]{2,1,0:T(8,128)S(1)} %project.1.coef_ref), channel_id=1, source_target_pairs={{0,28},{2,30},{4,0},{6,2},{8,4},{10,6},{12,8},{14,10},{16,12},{18,... | collective-permute-start | bytes 24584 | tf_op jit(solution)/shard_map/ppermute | solution.py:21
  49.5 16.0 %collective-permute-done = f32[2,8,128]{2,1,0:T(8,128)S(1)} collective-permute-done((f32[2,8,128]{2,1,0:T(8,128)S(1)}, f32[2,8,128]{2,1,0:T(8,128)S(1)}, u32[]{:S(2)}, u32[]{:S(2)}) %collective-permute-start) | collective-permute-done | bytes 8224 | tf_op jit(solution)/shard_map/ppermute | solution.py:21
  65.5 0.0 collective-permute-done.1
  65.5 0.6 collective-permute-done.2
  66.1 0.0 collective-permute-done.3
  66.1 10.5 %spread.1.local_ref = f32[16,144,128]{2,1,0:T(8,128)S(1)} custom-call(f32[16,144,128]{2,1,0:T(8,128)S(1)} %get-tuple-element.5.local_ref, f32[34,16,128]{2,1,0:T(8,128)S(1)} %bitcast.8, f32[2,8,128]{2,1,0:T(8,128)S(1)} %add_add_fusion.coef_ref, s32[3,128]{1,0:T(4,128)S(1)} %copy-done.5, s32[128]{0:T(128)S(1)} %copy-done.6), custom_call_target="tpu_custom_call" | custom-call | flops 10485760 | bytes 20971520 | tf_op jit(solution)/shard_map/spread/pallas_call | solution.py:355
  76.6 0.0 collective-permute-done.4
  76.6 0.7 add.21
  77.4 0.0 all-to-all-done.1.along_ref
  77.4 1.2 %finish.1 = f32[2,1,8,128,128]{4,3,2,1,0:T(8,128)} custom-call(f32[16,144,128]{2,1,0:T(8,128)S(1)} %spread.1.local_ref, f32[16,2,64,128]{3,2,1,0:T(8,128)S(1)} %all-to-all-done.1.along_ref), custom_call_target="tpu_custom_call" | custom-call | flops 1048576 | bytes 3145728 | tf_op jit(solution)/shard_map/finish/pallas_call | solution.py:368
  (2 shorter events, 0.0 us)
Async XLA Ops:
  0.6 1.2 %copy-start = (f32[2,1,8,128,128]{4,3,2,1,0:T(8,128)S(1)}, f32[2,1,8,128,128]{4,3,2,1,0:T(8,128)}, u32[]{:S(2)}) copy-start(f32[2,1,8,128,128]{4,3,2,1,0:T(8,128)} %wave_ref.5) | copy-start | bytes 3145732
  1.9 7.4 %copy-start.7 = (f32[2,16,8,256]{3,2,1,0:T(8,128)S(1)}, f32[2,16,8,256]{3,2,1,0:T(8,128)}, u32[]{:S(2)}) copy-start(f32[2,16,8,256]{3,2,1,0:T(8,128)} %param.13) | copy-start | bytes 786436
  3.1 31.3 %all-to-all-start = ((f32[16,2,64,128]{3,2,1,0:T(8,128)}), f32[16,2,64,128]{3,2,1,0:T(8,128)S(1)}, u32[]{:S(2)}, u32[]{:S(2)}) async-start(f32[16,2,64,128]{3,2,1,0:T(8,128)} %pack.1), calls=%async_computation | async-start | bytes 2097152 | tf_op jit(solution)/shard_map/all_to_all | solution.py:308
  12.1 2.3 %copy-start.1 = (f32[2,1,8,128,128]{4,3,2,1,0:T(8,128)S(1)}, f32[2,1,8,128,128]{4,3,2,1,0:T(8,128)}, u32[]{:S(2)}) copy-start(f32[2,1,8,128,128]{4,3,2,1,0:T(8,128)} %wave_ref.5) | copy-start | bytes 3145732
  12.1 2.3 %copy-start.4 = (f32[2,8,8]{2,1,0:T(8,128)S(1)}, f32[2,8,8]{2,1,0:T(8,128)}, u32[]{:S(2)}) copy-start(f32[2,8,8]{2,1,0:T(8,128)} %coupling_ref.1) | copy-start | bytes 1540
  12.1 2.3 %copy-start.5 = (s32[3,128]{1,0:T(4,128)S(1)}, s32[3,128]{1,0:T(4,128)}, u32[]{:S(2)}) copy-start(s32[3,128]{1,0:T(4,128)} %centres_ref.3) | copy-start | bytes 4612
  12.1 2.3 %copy-start.6 = (s32[128]{0:T(128)S(1)}, s32[128]{0:T(128)}, u32[]{:S(2)}) copy-start(s32[128]{0:T(128)} %species_ref.3) | copy-start | bytes 1540
  12.1 22.3 %copy-start.3 = (bf16[2,128,128]{2,1,0:T(8,128)(2,1)S(1)}, bf16[2,128,128]{2,1,0:T(8,128)(2,1)}, u32[]{:S(2)}) copy-start(bf16[2,128,128]{2,1,0:T(8,128)(2,1)} %constant.5.clone.matrix_ref) | copy-start | bytes 196612
  20.0 21.3 %copy-start.2 = (f32[8,128,128]{2,1,0:T(8,128)S(1)}, f32[8,128,128]{2,1,0:T(8,128)}, u32[]{:S(2)}) copy-start(f32[8,128,128]{2,1,0:T(8,128)} %potential_ref.1) | copy-start | bytes 1572868
  36.0 41.4 %all-to-all-start.1 = ((f32[16,2,64,128]{3,2,1,0:T(8,128)}), f32[16,2,64,128]{3,2,1,0:T(8,128)S(1)}, u32[]{:S(2)}, u32[]{:S(2)}) async-start(f32[16,2,64,128]{3,2,1,0:T(8,128)} %along_x.1), calls=%async_computation.1 | async-start | bytes 2097152 | tf_op jit(solution)/shard_map/all_to_all | solution.py:354
  42.3 34.3 %collective-permute-start.4 = (f32[8,64,128]{2,1,0:T(8,128)S(1)}, f32[8,64,128]{2,1,0:T(8,128)S(1)}, u32[]{:S(2)}, u32[]{:S(2)}) collective-permute-start(f32[8,64,128]{2,1,0:T(8,128)S(1)} %get-tuple-element.7), channel_id=1, source_target_pairs={{0,1},{1,0},{2,3},{3,2},{4,5},{5,4},{6,7},{7,6},{8,9},{9,8},{10,11... | collective-permute-start | bytes 786440 | tf_op jit(solution)/shard_map/ppermute | solution.py:21
  43.9 21.6 %collective-permute-start = (f32[2,8,128]{2,1,0:T(8,128)S(1)}, f32[2,8,128]{2,1,0:T(8,128)S(1)}, u32[]{:S(2)}, u32[]{:S(2)}) collective-permute-start(f32[2,8,128]{2,1,0:T(8,128)S(1)} %project.1.coef_ref), channel_id=1, source_target_pairs={{0,2},{2,4},{4,6},{6,8},{8,10},{10,12},{12,14},{14,16},{16,18},{18... | collective-permute-start | bytes 24584 | tf_op jit(solution)/shard_map/ppermute | solution.py:21
  43.9 21.6 %collective-permute-start.1 = (f32[2,8,128]{2,1,0:T(8,128)S(1)}, f32[2,8,128]{2,1,0:T(8,128)S(1)}, u32[]{:S(2)}, u32[]{:S(2)}) collective-permute-start(f32[2,8,128]{2,1,0:T(8,128)S(1)} %project.1.coef_ref), channel_id=1, source_target_pairs={{0,30},{2,0},{4,2},{6,4},{8,6},{10,8},{12,10},{14,12},{16,14},{18,... | collective-permute-start | bytes 24584 | tf_op jit(solution)/shard_map/ppermute | solution.py:21
  46.6 19.5 %collective-permute-start.2 = (f32[2,8,128]{2,1,0:T(8,128)S(1)}, f32[2,8,128]{2,1,0:T(8,128)S(1)}, u32[]{:S(2)}, u32[]{:S(2)}) collective-permute-start(f32[2,8,128]{2,1,0:T(8,128)S(1)} %project.1.coef_ref), channel_id=1, source_target_pairs={{0,4},{2,6},{4,8},{6,10},{8,12},{10,14},{12,16},{14,18},{16,20},{1... | collective-permute-start | bytes 24584 | tf_op jit(solution)/shard_map/ppermute | solution.py:21
  47.1 18.9 %collective-permute-start.3 = (f32[2,8,128]{2,1,0:T(8,128)S(1)}, f32[2,8,128]{2,1,0:T(8,128)S(1)}, u32[]{:S(2)}, u32[]{:S(2)}) collective-permute-start(f32[2,8,128]{2,1,0:T(8,128)S(1)} %project.1.coef_ref), channel_id=1, source_target_pairs={{0,28},{2,30},{4,0},{6,2},{8,4},{10,6},{12,8},{14,10},{16,12},{18,... | collective-permute-start | bytes 24584 | tf_op jit(solution)/shard_map/ppermute | solution.py:21

commit v4 on v3

--- a/solution.py
+++ b/solution.py
@@ -325,7 +325,6 @@
         name="project",
     )(wave, table, coupling, kinds, centres, species)
     reach = (box + planes - 2) // planes
-    own_coef = coef
     coef = coef + sum(
         passed_along(coef, "grid", step) for hop in range(reach) for step in (hop + 1, -hop - 1)
     )
@@ -350,7 +349,7 @@
         compiler_params=params(),
         cost_estimate=cost(6 * extent * wave.size, 2 * size),
         name="along_x",
-    )(held, matrix, own_coef)
+    )(held, matrix, coef)
     back = lax.all_to_all(along, "grid", 0, 0, tiled=True)
     local = pl.pallas_call(
         spread_kernel,

time: 79.1 us -> 68.3 us (0.86)
  waiting for transfers between devices: 31 us -> 17.7 us
  local copies, waits for them, and re-layouts: 6.39 us -> 9.33 us
  Pallas kernels: 21.1 us -> 20.2 us
    all_to_all x1, waiting for transfers between devices: 14.4 us -> 0.01 us  [per_device(): held = lax.all_to_all(send, 'grid', 0, 0, tiled=True)]
    all_to_all x1, waiting for transfers between devices: 0.01 us -> 11.2 us  [per_device(): back = lax.all_to_all(along, 'grid', 0, 0, tiled=True)]
    ppermute x5, waiting for transfers between devices: 16.6 us -> 6.41 us  [passed_along(): return lax.ppermute(value, axis, pairs)]
    transpose x1, local copies, waits for them, and re-layouts: 2.22 us -> 3.79 us  [per_device(): jnp.transpose(table, (0, 1, 3, 2, 4)).reshape(kind_count, box, box, lanes)]
    reshape x1, local copies, waits for them, and re-layouts: 0.63 us -> 2 us  [per_device(): table = projectors.reshape(kind_count, box, proj_count, box, box)]
  transfers between devices with their start and end apart: 7 -> 7, of which waited for: 3 -> 3; matrix products, arithmetic and copies ran while one was open for 7% -> 13% of each run, Pallas kernels for 22% -> 24%
where the time goes in v4:
time: 68.3 us; the launch traced here: 67.8 us
  Pallas kernels  20.2 us (30%)
  starting transfers between devices  18.4 us (27%)
  waiting for transfers between devices  17.7 us (26%)
  local copies, waits for them, and re-layouts  9.33 us (14%)
  between operations  1.42 us (2%)
  other arithmetic  0.74 us (1%)
    all_to_all x1, waiting for transfers between devices, per_device(): back = lax.all_to_all(along, 'grid', 0, 0, tiled=True)  11.2 us
    pallas_call x1, Pallas kernels, per_device(): pl.pallas_call(spread_kernel, out_shape=shape(local.shape), in_specs=[VME...  9.89 us
    ppermute x5, starting transfers between devices, passed_along(): return lax.ppermute(value, axis, pairs)  7.17 us
    ppermute x5, waiting for transfers between devices, passed_along(): return lax.ppermute(value, axis, pairs)  6.41 us
    all_to_all x1, starting transfers between devices, per_device(): held = lax.all_to_all(send, 'grid', 0, 0, tiled=True)  6.16 us
    pallas_call x1, Pallas kernels, per_device(): pl.pallas_call(project_kernel, out_shape=shape((rows, proj_count, atom_co...  5.28 us
    all_to_all x1, starting transfers between devices, per_device(): back = lax.all_to_all(along, 'grid', 0, 0, tiled=True)  5.09 us
    transpose x1, local copies, waits for them, and re-layouts, per_device(): jnp.transpose(table, (0, 1, 3, 2, 4)).reshape(kind_count, box, box, lanes)  3.79 us
  transfers between devices with their start and end apart: 7, of which 3 were waited for; matrix products, arithmetic and copies ran while one was open for 13% of the time, Pallas kernels for 24%

profile of v4, /device:TPU:16, one launch (start us, length us, event | category | flops | bytes accessed | tf_op | source)
XLA Modules:
  0.0 67.8 jit_solution(4751234093774174763)
XLA Ops:
  0.6 0.0 copy-start
  0.6 1.2 %copy-done = f32[2,1,8,128,128]{4,3,2,1,0:T(8,128)S(1)} copy-done((f32[2,1,8,128,128]{4,3,2,1,0:T(8,128)S(1)}, f32[2,1,8,128,128]{4,3,2,1,0:T(8,128)}, u32[]{:S(2)}) %copy-start) | copy-done | bytes 1048600
  1.9 0.0 copy-start.7
  1.9 1.2 %pack.1 = f32[16,2,64,128]{3,2,1,0:T(8,128)} custom-call(f32[2,1,8,128,128]{4,3,2,1,0:T(8,128)S(1)} %copy-done), custom_call_target="tpu_custom_call" | custom-call | flops 262144 | bytes 2097152 | tf_op jit(solution)/shard_map/pack/pallas_call | solution.py:299
  3.1 6.2 %all-to-all-start = ((f32[16,2,64,128]{3,2,1,0:T(8,128)}), f32[16,2,64,128]{3,2,1,0:T(8,128)S(1)}, u32[]{:S(2)}, u32[]{:S(2)}) async-start(f32[16,2,64,128]{3,2,1,0:T(8,128)} %pack.1), calls=%async_computation | async-start | bytes 2097152 | tf_op jit(solution)/shard_map/all_to_all | solution.py:308
  9.3 0.0 copy-done.7
  9.3 2.0 %reshape.16 = f32[2,16,8,16,16]{4,3,2,1,0:T(8,128)} reshape(f32[2,16,8,256]{3,2,1,0:T(8,128)S(1)} %copy-done.7) | data formatting | bytes 524288 | tf_op jit(solution)/shard_map/reshape | solution.py:309
  11.3 3.8 %copy.10 = f32[2,16,16,8,16]{4,3,2,1,0:T(8,128)} copy(f32[2,16,16,8,16]{4,2,3,1,0:T(8,128)} %bitcast.10) | data formatting | bytes 524288 | tf_op jit(solution)/shard_map/transpose | solution.py:310
  15.1 0.0 copy-start.1
  15.1 0.0 copy-start.4
  15.1 0.0 copy-start.5
  15.1 0.0 copy-start.6
  15.1 0.0 copy-start.3
  15.1 2.3 %reshape.17 = f32[2,16,16,128]{3,2,1,0:T(8,128)S(1)} reshape(f32[2,16,16,8,16]{4,3,2,1,0:T(8,128)} %copy.10) | data formatting | bytes 524288 | tf_op jit(solution)/shard_map/reshape | solution.py:310
  17.4 0.0 copy-done.1
  17.4 0.0 copy-done.4
  17.4 0.0 copy-done.5
  17.4 0.0 copy-done.6
  17.4 5.3 %project.1 = f32[2,8,128]{2,1,0:T(8,128)S(1)} custom-call(f32[2,1,8,128,128]{4,3,2,1,0:T(8,128)S(1)} %copy-done.1, f32[34,16,128]{2,1,0:T(8,128)S(1)} %bitcast.7, f32[2,8,8]{2,1,0:T(8,128)S(1)} %copy-done.4, s32[1,128]{1,0:T(1,128)S(1)} %bitcast.9, s32[3,128]{1,0:T(4,128)S(1)} %copy-done.5, s32[128]{0:T(128)S(1)} %copy-done.6), custom_call_target="tpu_custom_call" | custom-call | flops 10485760 | bytes 20971520 | tf_op jit(solution)/shard_map/project/pallas_call | solution.py:313
  22.7 0.3 collective-permute-start
  23.0 2.4 %collective-permute-start.1 = (f32[2,8,128]{2,1,0:T(8,128)S(1)}, f32[2,8,128]{2,1,0:T(8,128)S(1)}, u32[]{:S(2)}, u32[]{:S(2)}) collective-permute-start(f32[2,8,128]{2,1,0:T(8,128)S(1)} %project.1), channel_id=1, source_target_pairs={{0,30},{2,0},{4,2},{6,4},{8,6},{10,8},{12,10},{14,12},{16,14},{18,... | collective-permute-start | bytes 24584 | tf_op jit(solution)/shard_map/ppermute | solution.py:21
  25.4 0.0 collective-permute-start.2
  25.4 2.9 %collective-permute-start.3 = (f32[2,8,128]{2,1,0:T(8,128)S(1)}, f32[2,8,128]{2,1,0:T(8,128)S(1)}, u32[]{:S(2)}, u32[]{:S(2)}) collective-permute-start(f32[2,8,128]{2,1,0:T(8,128)S(1)} %project.1), channel_id=1, source_target_pairs={{0,28},{2,30},{4,0},{6,2},{8,4},{10,6},{12,8},{14,10},{16,12},{18,... | collective-permute-start | bytes 24584 | tf_op jit(solution)/shard_map/ppermute | solution.py:21
  28.3 5.8 %collective-permute-done = f32[2,8,128]{2,1,0:T(8,128)S(1)} collective-permute-done((f32[2,8,128]{2,1,0:T(8,128)S(1)}, f32[2,8,128]{2,1,0:T(8,128)S(1)}, u32[]{:S(2)}, u32[]{:S(2)}) %collective-permute-start) | collective-permute-done | bytes 8224 | tf_op jit(solution)/shard_map/ppermute | solution.py:21
  34.1 0.0 collective-permute-done.1
  34.1 0.6 collective-permute-done.2
  34.7 0.0 collective-permute-done.3
  34.7 0.0 copy-start.2
  34.7 0.0 all-to-all-done.held_ref
  34.7 0.0 copy-done.3
  34.7 1.5 %along_x.1 = f32[16,2,64,128]{3,2,1,0:T(8,128)} custom-call(f32[16,2,64,128]{3,2,1,0:T(8,128)S(1)} %all-to-all-done.held_ref, bf16[2,128,128]{2,1,0:T(8,128)(2,1)S(1)} %copy-done.3, f32[2,8,128]{2,1,0:T(8,128)S(1)} %add_add_fusion.coef_ref), custom_call_target="tpu_custom_call" | custom-call | flops 201326592 | bytes 2097152 | tf_op jit(solution)/shard_map/along_x/pallas_call | solution.py:343
  36.3 5.1 %all-to-all-start.1 = ((f32[16,2,64,128]{3,2,1,0:T(8,128)}), f32[16,2,64,128]{3,2,1,0:T(8,128)S(1)}, u32[]{:S(2)}, u32[]{:S(2)}) async-start(f32[16,2,64,128]{3,2,1,0:T(8,128)} %along_x.1), calls=%async_computation.1 | async-start | bytes 2097152 | tf_op jit(solution)/shard_map/all_to_all | solution.py:353
  42.0 0.0 copy-done.2
  42.0 1.0 %local.1 = (f32[16,144,128]{2,1,0:T(8,128)S(1)}, f32[8,64,128]{2,1,0:T(8,128)S(1)}, f32[8,64,128]{2,1,0:T(8,128)S(1)}) custom-call(f32[2,1,8,128,128]{4,3,2,1,0:T(8,128)S(1)} %copy-done.1, f32[8,128,128]{2,1,0:T(8,128)S(1)} %copy-done.2, bf16[2,128,128]{2,1,0:T(8,128)(2,1)S(1)} %copy-done.3, f32[1]{0:T(128)S(6)} %copy.11.occ_ref), custom_call_target="tpu_custom_call" | custom-call | flops 402653184 | bytes 3145728 | tf_op jit(solution)/shard_map/local/pallas_call | solution.py:331
  43.1 1.6 %collective-permute-start.4 = (f32[8,64,128]{2,1,0:T(8,128)S(1)}, f32[8,64,128]{2,1,0:T(8,128)S(1)}, u32[]{:S(2)}, u32[]{:S(2)}) collective-permute-start(f32[8,64,128]{2,1,0:T(8,128)S(1)} %get-tuple-element.7), channel_id=1, source_target_pairs={{0,1},{1,0},{2,3},{3,2},{4,5},{5,4},{6,7},{7,6},{8,9},{9,8},{10,11... | collective-permute-start | bytes 786440 | tf_op jit(solution)/shard_map/ppermute | solution.py:21
  44.7 9.9 %spread.1.local_ref = f32[16,144,128]{2,1,0:T(8,128)S(1)} custom-call(f32[16,144,128]{2,1,0:T(8,128)S(1)} %get-tuple-element.5.local_ref, f32[34,16,128]{2,1,0:T(8,128)S(1)} %bitcast.8, f32[2,8,128]{2,1,0:T(8,128)S(1)} %add_add_fusion.coef_ref, s32[3,128]{1,0:T(4,128)S(1)} %copy-done.5, s32[128]{0:T(128)S(1)} %copy-done.6), custom_call_target="tpu_custom_call" | custom-call | flops 10485760 | bytes 20971520 | tf_op jit(solution)/shard_map/spread/pallas_call | solution.py:354
  54.6 0.0 collective-permute-done.4
  54.6 0.7 %add.21 = f32[8,64,128]{2,1,0:T(8,128)} add(f32[8,64,128]{2,1,0:T(8,128)S(1)} %get-tuple-element.6, f32[8,64,128]{2,1,0:T(8,128)S(1)} %collective-permute-done.4) | non-fusion elementwise | flops 65536 | bytes 786432 | tf_op jit(solution)/shard_map/add | solution.py:342
  55.3 11.2 %all-to-all-done.1.along_ref = f32[16,2,64,128]{3,2,1,0:T(8,128)S(1)} async-done(((f32[16,2,64,128]{3,2,1,0:T(8,128)}), f32[16,2,64,128]{3,2,1,0:T(8,128)S(1)}, u32[]{:S(2)}, u32[]{:S(2)}) %all-to-all-start.1) | async-done | bytes 1048608 | tf_op jit(solution)/shard_map/all_to_all | solution.py:353
  66.6 1.2 %finish.1 = f32[2,1,8,128,128]{4,3,2,1,0:T(8,128)} custom-call(f32[16,144,128]{2,1,0:T(8,128)S(1)} %spread.1.local_ref, f32[16,2,64,128]{3,2,1,0:T(8,128)S(1)} %all-to-all-done.1.along_ref), custom_call_target="tpu_custom_call" | custom-call | flops 1048576 | bytes 3145728 | tf_op jit(solution)/shard_map/finish/pallas_call | solution.py:367
  (2 shorter events, 0.0 us)
Async XLA Ops:
  0.6 1.2 %copy-start = (f32[2,1,8,128,128]{4,3,2,1,0:T(8,128)S(1)}, f32[2,1,8,128,128]{4,3,2,1,0:T(8,128)}, u32[]{:S(2)}) copy-start(f32[2,1,8,128,128]{4,3,2,1,0:T(8,128)} %wave_ref.5) | copy-start | bytes 3145732
  1.9 7.4 %copy-start.7 = (f32[2,16,8,256]{3,2,1,0:T(8,128)S(1)}, f32[2,16,8,256]{3,2,1,0:T(8,128)}, u32[]{:S(2)}) copy-start(f32[2,16,8,256]{3,2,1,0:T(8,128)} %param.13) | copy-start | bytes 786436
  3.1 31.6 %all-to-all-start = ((f32[16,2,64,128]{3,2,1,0:T(8,128)}), f32[16,2,64,128]{3,2,1,0:T(8,128)S(1)}, u32[]{:S(2)}, u32[]{:S(2)}) async-start(f32[16,2,64,128]{3,2,1,0:T(8,128)} %pack.1), calls=%async_computation | async-start | bytes 2097152 | tf_op jit(solution)/shard_map/all_to_all | solution.py:308
  15.1 2.3 %copy-start.1 = (f32[2,1,8,128,128]{4,3,2,1,0:T(8,128)S(1)}, f32[2,1,8,128,128]{4,3,2,1,0:T(8,128)}, u32[]{:S(2)}) copy-start(f32[2,1,8,128,128]{4,3,2,1,0:T(8,128)} %wave_ref.5) | copy-start | bytes 3145732
  15.1 2.3 %copy-start.4 = (f32[2,8,8]{2,1,0:T(8,128)S(1)}, f32[2,8,8]{2,1,0:T(8,128)}, u32[]{:S(2)}) copy-start(f32[2,8,8]{2,1,0:T(8,128)} %coupling_ref.1) | copy-start | bytes 1540
  15.1 2.3 %copy-start.5 = (s32[3,128]{1,0:T(4,128)S(1)}, s32[3,128]{1,0:T(4,128)}, u32[]{:S(2)}) copy-start(s32[3,128]{1,0:T(4,128)} %centres_ref.3) | copy-start | bytes 4612
  15.1 2.3 %copy-start.6 = (s32[128]{0:T(128)S(1)}, s32[128]{0:T(128)}, u32[]{:S(2)}) copy-start(s32[128]{0:T(128)} %species_ref.3) | copy-start | bytes 1540
  15.1 19.7 %copy-start.3 = (bf16[2,128,128]{2,1,0:T(8,128)(2,1)S(1)}, bf16[2,128,128]{2,1,0:T(8,128)(2,1)}, u32[]{:S(2)}) copy-start(bf16[2,128,128]{2,1,0:T(8,128)(2,1)} %constant.5.clone.matrix_ref) | copy-start | bytes 196612
  22.7 11.4 %collective-permute-start = (f32[2,8,128]{2,1,0:T(8,128)S(1)}, f32[2,8,128]{2,1,0:T(8,128)S(1)}, u32[]{:S(2)}, u32[]{:S(2)}) collective-permute-start(f32[2,8,128]{2,1,0:T(8,128)S(1)} %project.1), channel_id=1, source_target_pairs={{0,2},{2,4},{4,6},{6,8},{8,10},{10,12},{12,14},{14,16},{16,18},{18... | collective-permute-start | bytes 24584 | tf_op jit(solution)/shard_map/ppermute | solution.py:21
  23.0 11.1 %collective-permute-start.1 = (f32[2,8,128]{2,1,0:T(8,128)S(1)}, f32[2,8,128]{2,1,0:T(8,128)S(1)}, u32[]{:S(2)}, u32[]{:S(2)}) collective-permute-start(f32[2,8,128]{2,1,0:T(8,128)S(1)} %project.1), channel_id=1, source_target_pairs={{0,30},{2,0},{4,2},{6,4},{8,6},{10,8},{12,10},{14,12},{16,14},{18,... | collective-permute-start | bytes 24584 | tf_op jit(solution)/shard_map/ppermute | solution.py:21
  25.4 9.3 %collective-permute-start.2 = (f32[2,8,128]{2,1,0:T(8,128)S(1)}, f32[2,8,128]{2,1,0:T(8,128)S(1)}, u32[]{:S(2)}, u32[]{:S(2)}) collective-permute-start(f32[2,8,128]{2,1,0:T(8,128)S(1)} %project.1), channel_id=1, source_target_pairs={{0,4},{2,6},{4,8},{6,10},{8,12},{10,14},{12,16},{14,18},{16,20},{1... | collective-permute-start | bytes 24584 | tf_op jit(solution)/shard_map/ppermute | solution.py:21
  25.4 9.3 %collective-permute-start.3 = (f32[2,8,128]{2,1,0:T(8,128)S(1)}, f32[2,8,128]{2,1,0:T(8,128)S(1)}, u32[]{:S(2)}, u32[]{:S(2)}) collective-permute-start(f32[2,8,128]{2,1,0:T(8,128)S(1)} %project.1), channel_id=1, source_target_pairs={{0,28},{2,30},{4,0},{6,2},{8,4},{10,6},{12,8},{14,10},{16,12},{18,... | collective-permute-start | bytes 24584 | tf_op jit(solution)/shard_map/ppermute | solution.py:21
  34.7 7.3 %copy-start.2 = (f32[8,128,128]{2,1,0:T(8,128)S(1)}, f32[8,128,128]{2,1,0:T(8,128)}, u32[]{:S(2)}) copy-start(f32[8,128,128]{2,1,0:T(8,128)} %potential_ref.1) | copy-start | bytes 1572868
  36.3 30.3 %all-to-all-start.1 = ((f32[16,2,64,128]{3,2,1,0:T(8,128)}), f32[16,2,64,128]{3,2,1,0:T(8,128)S(1)}, u32[]{:S(2)}, u32[]{:S(2)}) async-start(f32[16,2,64,128]{3,2,1,0:T(8,128)} %along_x.1), calls=%async_computation.1 | async-start | bytes 2097152 | tf_op jit(solution)/shard_map/all_to_all | solution.py:353
  43.1 11.5 %collective-permute-start.4 = (f32[8,64,128]{2,1,0:T(8,128)S(1)}, f32[8,64,128]{2,1,0:T(8,128)S(1)}, u32[]{:S(2)}, u32[]{:S(2)}) collective-permute-start(f32[8,64,128]{2,1,0:T(8,128)S(1)} %get-tuple-element.7), channel_id=1, source_target_pairs={{0,1},{1,0},{2,3},{3,2},{4,5},{5,4},{6,7},{7,6},{8,9},{9,8},{10,11... | collective-permute-start | bytes 786440 | tf_op jit(solution)/shard_map/ppermute | solution.py:21

commit v5 on v3

--- a/solution.py
+++ b/solution.py
@@ -1,3 +1,4 @@
+import functools
 import math
 
 import jax
@@ -50,17 +51,16 @@
     return dot(left[0], right[0]) + (dot(left[0], right[1]) + dot(left[1], right[0]))
 
 
-def pack_kernel(wave_ref, send_ref):
+def pack_kernel(c, wave_ref, send_ref):
     _, orbitals, planes, extent, _ = wave_ref.shape
     count = send_ref.shape[0]
     width = extent // count
     for p in range(planes):
-        for c in range(2):
-            for o in range(orbitals):
-                for d in range(count):
-                    send_ref[d, c * orbitals + o, pl.ds(p, width, stride=planes), :] = wave_ref[
-                        c, o, p, d * width : (d + 1) * width, :
-                    ]
+        for o in range(orbitals):
+            for d in range(count):
+                send_ref[d, o, pl.ds(p, width, stride=planes), :] = wave_ref[
+                    c, o, p, d * width : (d + 1) * width, :
+                ]
 
 
 def along_x_kernel(held_ref, matrix_ref, coef_ref, out_ref, lined):
@@ -252,21 +252,22 @@
     lax.fori_loop(0, found, one, 0)
 
 
-def finish_kernel(local_ref, along_ref, out_ref):
+def finish_kernel(local_ref, real_ref, imag_ref, out_ref):
     _, orbitals, planes, extent, _ = out_ref.shape
-    count = along_ref.shape[0]
+    count = real_ref.shape[0]
     width = extent // count
     box = local_ref.shape[1] - extent
     half_step = 0.5 * time_step
     for c in range(2):
         factor = half_step if c == 1 else -half_step
+        along_ref = (real_ref, imag_ref)[c]
         for o in range(orbitals):
             r = c * orbitals + o
             for p in range(planes):
                 for d in range(count):
                     total = (
                         local_ref[r * planes + p, d * width : (d + 1) * width, :]
-                        + along_ref[d, r, pl.ds(p, width, stride=planes), :]
+                        + along_ref[d, o, pl.ds(p, width, stride=planes), :]
                     )
                     if d * width < box:
                         total += local_ref[
@@ -296,16 +297,18 @@
     kinds = species.reshape(1, atom_count)
     shares = lax.axis_size("orb")
     density_shape = shape((planes, extent // shares, extent))
-    send = pl.pallas_call(
-        pack_kernel,
-        out_shape=shape((count, rows, width * planes, extent)),
-        in_specs=[VMEM],
-        out_specs=VMEM,
-        compiler_params=params(),
-        cost_estimate=cost(wave.size, 2 * size),
-        name="pack",
-    )(wave)
-    held = lax.all_to_all(send, "grid", 0, 0, tiled=True)
+    held = []
+    for c in range(2):
+        send = pl.pallas_call(
+            functools.partial(pack_kernel, c),
+            out_shape=shape((count, orbitals, width * planes, extent)),
+            in_specs=[VMEM],
+            out_specs=VMEM,
+            compiler_params=params(),
+            cost_estimate=cost(wave.size, size),
+            name="pack",
+        )(wave)
+        held.append(lax.all_to_all(send, "grid", 0, 0, tiled=True))
     table = projectors.reshape(kind_count, box, proj_count, box, box)
     table = jnp.transpose(table, (0, 1, 3, 2, 4)).reshape(kind_count, box, box, lanes)
     table = jnp.pad(table, ((0, 0), (0, 1), (0, 0), (0, 0)))
@@ -341,17 +344,19 @@
     density = terms[0]
     for k in range(1, shares):
         density = density + passed_along(terms[k], "orb", k)
-    along = pl.pallas_call(
-        along_x_kernel,
-        out_shape=shape(held.shape),
-        in_specs=[VMEM, VMEM, pl.BlockSpec(memory_space=pl.ANY)],
-        out_specs=VMEM,
-        scratch_shapes=[pltpu.VMEM((extent, extent), jnp.float32)],
-        compiler_params=params(),
-        cost_estimate=cost(6 * extent * wave.size, 2 * size),
-        name="along_x",
-    )(held, matrix, own_coef)
-    back = lax.all_to_all(along, "grid", 0, 0, tiled=True)
+    back = []
+    for c in range(2):
+        along = pl.pallas_call(
+            along_x_kernel,
+            out_shape=shape(held[c].shape),
+            in_specs=[VMEM, VMEM, pl.BlockSpec(memory_space=pl.ANY)],
+            out_specs=VMEM,
+            scratch_shapes=[pltpu.VMEM((extent, extent), jnp.float32)],
+            compiler_params=params(),
+            cost_estimate=cost(3 * extent * wave.size, size),
+            name="along_x",
+        )(held[c], matrix, own_coef if c == 0 else coef)
+        back.append(lax.all_to_all(along, "grid", 0, 0, tiled=True))
     local = pl.pallas_call(
         spread_kernel,
         out_shape=shape(local.shape),
@@ -368,12 +373,12 @@
     update = pl.pallas_call(
         finish_kernel,
         out_shape=shape(wave.shape),
-        in_specs=[VMEM, VMEM],
+        in_specs=[VMEM] * 3,
         out_specs=VMEM,
         compiler_params=params(),
         cost_estimate=cost(4 * wave.size, 3 * size),
         name="finish",
-    )(local, back)
+    )(local, *back)
     return (update, density)
 
 

time: 79.1 us -> 95.7 us (1.21)
  the two profiles are of different devices: /device:TPU:16 before, /device:TPU:0 now
where the time goes in v5:
time: 95.7 us; the launch traced here: 94.2 us
  starting transfers between devices  32.6 us (34%)
  waiting for transfers between devices  30.3 us (32%)
  Pallas kernels  19.9 us (21%)
  local copies, waits for them, and re-layouts  9.26 us (10%)
  between operations  1.43 us (1%)
    all_to_all x2, waiting for transfers between devices, per_device(): back.append(lax.all_to_all(along, 'grid', 0, 0, tiled=True))  15.1 us
    all_to_all x2, waiting for transfers between devices, per_device(): held.append(lax.all_to_all(send, 'grid', 0, 0, tiled=True))  13.5 us
    all_to_all x2, starting transfers between devices, per_device(): held.append(lax.all_to_all(send, 'grid', 0, 0, tiled=True))  11.6 us
    ppermute x5, starting transfers between devices, passed_along(): return lax.ppermute(value, axis, pairs)  10.8 us
    all_to_all x2, starting transfers between devices, per_device(): back.append(lax.all_to_all(along, 'grid', 0, 0, tiled=True))  10.2 us
    pallas_call x1, Pallas kernels, per_device(): pl.pallas_call(spread_kernel, out_shape=shape(local.shape), in_specs=[VME...  8.61 us
    pallas_call x1, Pallas kernels, per_device(): pl.pallas_call(project_kernel, out_shape=shape((rows, proj_count, atom_co...  4.8 us
    transpose x1, local copies, waits for them, and re-layouts, per_device(): jnp.transpose(table, (0, 1, 3, 2, 4)).reshape(kind_count, box, box, lanes)  3.77 us
  transfers between devices with their start and end apart: 9, of which 4 were waited for; matrix products, arithmetic and copies ran while one was open for 9% of the time, Pallas kernels for 19%

profile of v5, /device:TPU:0, one launch (start us, length us, event | category | flops | bytes accessed | tf_op | source)
XLA Modules:
  0.0 94.2 jit_solution(1226361264084748555)
XLA Ops:
  0.6 0.0 copy-start
  0.6 1.2 %copy-done = f32[2,1,8,128,128]{4,3,2,1,0:T(8,128)S(1)} copy-done((f32[2,1,8,128,128]{4,3,2,1,0:T(8,128)S(1)}, f32[2,1,8,128,128]{4,3,2,1,0:T(8,128)}, u32[]{:S(2)}) %copy-start) | copy-done | bytes 1048600
  1.9 0.0 copy-start.1
  1.9 0.9 pack.3
  2.8 0.0 copy-start.7
  2.8 7.5 %all-to-all-start.2 = ((f32[16,1,64,128]{3,2,1,0:T(8,128)}), f32[16,1,64,128]{3,2,1,0:T(8,128)S(1)}, u32[]{:S(2)}, u32[]{:S(2)}) async-start(f32[16,1,64,128]{3,2,1,0:T(8,128)} %pack.3), calls=%async_computation.2 | async-start | bytes 1048576 | tf_op jit(solution)/shard_map/all_to_all | solution.py:311
  10.3 0.0 copy-done.1
  10.3 0.9 pack.2
  11.2 13.5 %all-to-all-done.2.held_ref = f32[16,1,64,128]{3,2,1,0:T(8,128)S(1)} async-done(((f32[16,1,64,128]{3,2,1,0:T(8,128)}), f32[16,1,64,128]{3,2,1,0:T(8,128)S(1)}, u32[]{:S(2)}, u32[]{:S(2)}) %all-to-all-start.2) | async-done | bytes 524320 | tf_op jit(solution)/shard_map/all_to_all | solution.py:311
  24.8 4.1 %all-to-all-start = ((f32[16,1,64,128]{3,2,1,0:T(8,128)}), f32[16,1,64,128]{3,2,1,0:T(8,128)S(1)}, u32[]{:S(2)}, u32[]{:S(2)}) async-start(f32[16,1,64,128]{3,2,1,0:T(8,128)} %pack.2), calls=%async_computation | async-start | bytes 1048576 | tf_op jit(solution)/shard_map/all_to_all | solution.py:311
  28.9 0.0 copy-done.7
  28.9 2.0 %reshape.16 = f32[2,16,8,16,16]{4,3,2,1,0:T(8,128)} reshape(f32[2,16,8,256]{3,2,1,0:T(8,128)S(1)} %copy-done.7) | data formatting | bytes 524288 | tf_op jit(solution)/shard_map/reshape | solution.py:312
  30.9 3.8 %copy.10 = f32[2,16,16,8,16]{4,3,2,1,0:T(8,128)} copy(f32[2,16,16,8,16]{4,2,3,1,0:T(8,128)} %bitcast.10) | data formatting | bytes 524288 | tf_op jit(solution)/shard_map/transpose | solution.py:313
  34.6 0.0 copy-start.4
  34.6 0.0 copy-start.5
  34.6 0.0 copy-start.6
  34.6 0.0 copy-start.2
  34.6 2.2 %reshape.17 = f32[2,16,16,128]{3,2,1,0:T(8,128)S(1)} reshape(f32[2,16,16,8,16]{4,3,2,1,0:T(8,128)} %copy.10) | data formatting | bytes 524288 | tf_op jit(solution)/shard_map/reshape | solution.py:313
  36.9 0.0 copy-done.4
  36.9 0.0 copy-done.5
  36.9 0.0 copy-done.6
  36.9 4.8 %project.1.coef_ref = f32[2,8,128]{2,1,0:T(8,128)S(1)} custom-call(f32[2,1,8,128,128]{4,3,2,1,0:T(8,128)S(1)} %copy-done.1, f32[34,16,128]{2,1,0:T(8,128)S(1)} %bitcast.7, f32[2,8,8]{2,1,0:T(8,128)S(1)} %copy-done.4, s32[1,128]{1,0:T(1,128)S(1)} %bitcast.9, s32[3,128]{1,0:T(4,128)S(1)} %copy-done.5, s32[128]{0:T(128)S(1)} %copy-done.6), custom_call_target="tpu_custom_call" | custom-call | flops 10485760 | bytes 20971520 | tf_op jit(solution)/shard_map/project/pallas_call | solution.py:316
  41.8 0.2 collective-permute-start
  41.9 4.3 %collective-permute-start.1 = (f32[2,8,128]{2,1,0:T(8,128)S(1)}, f32[2,8,128]{2,1,0:T(8,128)S(1)}, u32[]{:S(2)}, u32[]{:S(2)}) collective-permute-start(f32[2,8,128]{2,1,0:T(8,128)S(1)} %project.1.coef_ref), channel_id=1, source_target_pairs={{0,30},{2,0},{4,2},{6,4},{8,6},{10,8},{12,10},{14,12},{16,14},{18,... | collective-permute-start | bytes 24584 | tf_op jit(solution)/shard_map/ppermute | solution.py:22
  46.2 0.0 collective-permute-start.2
  46.2 4.7 %collective-permute-start.3 = (f32[2,8,128]{2,1,0:T(8,128)S(1)}, f32[2,8,128]{2,1,0:T(8,128)S(1)}, u32[]{:S(2)}, u32[]{:S(2)}) collective-permute-start(f32[2,8,128]{2,1,0:T(8,128)S(1)} %project.1.coef_ref), channel_id=1, source_target_pairs={{0,28},{2,30},{4,0},{6,2},{8,4},{10,6},{12,8},{14,10},{16,12},{18,... | collective-permute-start | bytes 24584 | tf_op jit(solution)/shard_map/ppermute | solution.py:22
  50.9 0.0 collective-permute-done
  50.9 0.0 collective-permute-done.1
  50.9 1.6 %collective-permute-done.2 = f32[2,8,128]{2,1,0:T(8,128)S(1)} collective-permute-done((f32[2,8,128]{2,1,0:T(8,128)S(1)}, f32[2,8,128]{2,1,0:T(8,128)S(1)}, u32[]{:S(2)}, u32[]{:S(2)}) %collective-permute-start.2) | collective-permute-done | bytes 8224 | tf_op jit(solution)/shard_map/ppermute | solution.py:22
  52.6 0.0 collective-permute-done.3
  52.6 0.0 copy-done.2
  52.6 0.0 copy-start.3
  52.6 1.2 %along_x.3 = f32[16,1,64,128]{3,2,1,0:T(8,128)} custom-call(f32[16,1,64,128]{3,2,1,0:T(8,128)S(1)} %all-to-all-done.2.held_ref, bf16[2,128,128]{2,1,0:T(8,128)(2,1)S(1)} %copy-done.2, f32[2,8,128]{2,1,0:T(8,128)S(1)} %add_add_fusion.coef_ref), custom_call_target="tpu_custom_call" | custom-call | flops 100663296 | bytes 1048576 | tf_op jit(solution)/shard_map/along_x/pallas_call | solution.py:349
  53.8 0.0 all-to-all-done.held_ref
  53.8 6.1 %all-to-all-start.3 = ((f32[16,1,64,128]{3,2,1,0:T(8,128)}), f32[16,1,64,128]{3,2,1,0:T(8,128)S(1)}, u32[]{:S(2)}, u32[]{:S(2)}) async-start(f32[16,1,64,128]{3,2,1,0:T(8,128)} %along_x.3), calls=%async_computation.3 | async-start | bytes 1048576 | tf_op jit(solution)/shard_map/all_to_all | solution.py:359
  59.9 1.2 %along_x.2 = f32[16,1,64,128]{3,2,1,0:T(8,128)} custom-call(f32[16,1,64,128]{3,2,1,0:T(8,128)S(1)} %all-to-all-done.held_ref, bf16[2,128,128]{2,1,0:T(8,128)(2,1)S(1)} %copy-done.2, f32[2,8,128]{2,1,0:T(8,128)S(1)} %project.1.coef_ref), custom_call_target="tpu_custom_call" | custom-call | flops 100663296 | bytes 1048576 | tf_op jit(solution)/shard_map/along_x/pallas_call | solution.py:349
  61.0 13.3 %all-to-all-done.3.imag_ref = f32[16,1,64,128]{3,2,1,0:T(8,128)S(1)} async-done(((f32[16,1,64,128]{3,2,1,0:T(8,128)}), f32[16,1,64,128]{3,2,1,0:T(8,128)S(1)}, u32[]{:S(2)}, u32[]{:S(2)}) %all-to-all-start.3) | async-done | bytes 524320 | tf_op jit(solution)/shard_map/all_to_all | solution.py:359
  74.3 4.1 %all-to-all-start.1 = ((f32[16,1,64,128]{3,2,1,0:T(8,128)}), f32[16,1,64,128]{3,2,1,0:T(8,128)S(1)}, u32[]{:S(2)}, u32[]{:S(2)}) async-start(f32[16,1,64,128]{3,2,1,0:T(8,128)} %along_x.2), calls=%async_computation.1 | async-start | bytes 1048576 | tf_op jit(solution)/shard_map/all_to_all | solution.py:359
  79.1 0.0 copy-done.3
  79.1 1.0 %local.1 = (f32[16,144,128]{2,1,0:T(8,128)S(1)}, f32[8,64,128]{2,1,0:T(8,128)S(1)}, f32[8,64,128]{2,1,0:T(8,128)S(1)}) custom-call(f32[2,1,8,128,128]{4,3,2,1,0:T(8,128)S(1)} %copy-done.1, f32[8,128,128]{2,1,0:T(8,128)S(1)} %copy-done.3, bf16[2,128,128]{2,1,0:T(8,128)(2,1)S(1)} %copy-done.2, f32[1]{0:T(128)S(6)} %copy.11.occ_ref), custom_call_target="tpu_custom_call" | custom-call | flops 402653184 | bytes 3145728 | tf_op jit(solution)/shard_map/local/pallas_call | solution.py:335
  80.2 1.6 %collective-permute-start.4 = (f32[8,64,128]{2,1,0:T(8,128)S(1)}, f32[8,64,128]{2,1,0:T(8,128)S(1)}, u32[]{:S(2)}, u32[]{:S(2)}) collective-permute-start(f32[8,64,128]{2,1,0:T(8,128)S(1)} %get-tuple-element.7), channel_id=1, source_target_pairs={{0,1},{1,0},{2,3},{3,2},{4,5},{5,4},{6,7},{7,6},{8,9},{9,8},{10,11... | collective-permute-start | bytes 786440 | tf_op jit(solution)/shard_map/ppermute | solution.py:22
  81.7 8.6 %spread.1.local_ref = f32[16,144,128]{2,1,0:T(8,128)S(1)} custom-call(f32[16,144,128]{2,1,0:T(8,128)S(1)} %get-tuple-element.5.local_ref, f32[34,16,128]{2,1,0:T(8,128)S(1)} %bitcast.8, f32[2,8,128]{2,1,0:T(8,128)S(1)} %add_add_fusion.coef_ref, s32[3,128]{1,0:T(4,128)S(1)} %copy-done.5, s32[128]{0:T(128)S(1)} %copy-done.6), custom_call_target="tpu_custom_call" | custom-call | flops 10485760 | bytes 20971520 | tf_op jit(solution)/shard_map/spread/pallas_call | solution.py:360
  90.4 0.0 collective-permute-done.4
  90.4 0.7 add.21
  91.1 1.8 %all-to-all-done.1.real_ref = f32[16,1,64,128]{3,2,1,0:T(8,128)S(1)} async-done(((f32[16,1,64,128]{3,2,1,0:T(8,128)}), f32[16,1,64,128]{3,2,1,0:T(8,128)S(1)}, u32[]{:S(2)}, u32[]{:S(2)}) %all-to-all-start.1) | async-done | bytes 524320 | tf_op jit(solution)/shard_map/all_to_all | solution.py:359
  92.9 1.2 %finish.1 = f32[2,1,8,128,128]{4,3,2,1,0:T(8,128)} custom-call(f32[16,144,128]{2,1,0:T(8,128)S(1)} %spread.1.local_ref, f32[16,1,64,128]{3,2,1,0:T(8,128)S(1)} %all-to-all-done.1.real_ref, f32[16,1,64,128]{3,2,1,0:T(8,128)S(1)} %all-to-all-done.3.imag_ref), custom_call_target="tpu_custom_call" | custom-call | flops 1048576 | bytes 3145728 | tf_op jit(solution)/shard_map/finish/pallas_call | solution.py:373
  (2 shorter events, 0.0 us)
Async XLA Ops:
  0.6 1.2 %copy-start = (f32[2,1,8,128,128]{4,3,2,1,0:T(8,128)S(1)}, f32[2,1,8,128,128]{4,3,2,1,0:T(8,128)}, u32[]{:S(2)}) copy-start(f32[2,1,8,128,128]{4,3,2,1,0:T(8,128)} %wave_ref.7) | copy-start | bytes 3145732
  1.9 8.4 %copy-start.1 = (f32[2,1,8,128,128]{4,3,2,1,0:T(8,128)S(1)}, f32[2,1,8,128,128]{4,3,2,1,0:T(8,128)}, u32[]{:S(2)}) copy-start(f32[2,1,8,128,128]{4,3,2,1,0:T(8,128)} %wave_ref.7) | copy-start | bytes 3145732
  2.8 26.1 %copy-start.7 = (f32[2,16,8,256]{3,2,1,0:T(8,128)S(1)}, f32[2,16,8,256]{3,2,1,0:T(8,128)}, u32[]{:S(2)}) copy-start(f32[2,16,8,256]{3,2,1,0:T(8,128)} %param.13) | copy-start | bytes 786436
  2.8 22.0 %all-to-all-start.2 = ((f32[16,1,64,128]{3,2,1,0:T(8,128)}), f32[16,1,64,128]{3,2,1,0:T(8,128)S(1)}, u32[]{:S(2)}, u32[]{:S(2)}) async-start(f32[16,1,64,128]{3,2,1,0:T(8,128)} %pack.3), calls=%async_computation.2 | async-start | bytes 1048576 | tf_op jit(solution)/shard_map/all_to_all | solution.py:311
  24.8 29.0 %all-to-all-start = ((f32[16,1,64,128]{3,2,1,0:T(8,128)}), f32[16,1,64,128]{3,2,1,0:T(8,128)S(1)}, u32[]{:S(2)}, u32[]{:S(2)}) async-start(f32[16,1,64,128]{3,2,1,0:T(8,128)} %pack.2), calls=%async_computation | async-start | bytes 1048576 | tf_op jit(solution)/shard_map/all_to_all | solution.py:311
  34.6 2.3 %copy-start.4 = (f32[2,8,8]{2,1,0:T(8,128)S(1)}, f32[2,8,8]{2,1,0:T(8,128)}, u32[]{:S(2)}) copy-start(f32[2,8,8]{2,1,0:T(8,128)} %coupling_ref.1) | copy-start | bytes 1540
  34.6 2.3 %copy-start.5 = (s32[3,128]{1,0:T(4,128)S(1)}, s32[3,128]{1,0:T(4,128)}, u32[]{:S(2)}) copy-start(s32[3,128]{1,0:T(4,128)} %centres_ref.3) | copy-start | bytes 4612
  34.6 2.3 %copy-start.6 = (s32[128]{0:T(128)S(1)}, s32[128]{0:T(128)}, u32[]{:S(2)}) copy-start(s32[128]{0:T(128)} %species_ref.3) | copy-start | bytes 1540
  34.6 17.9 %copy-start.2 = (bf16[2,128,128]{2,1,0:T(8,128)(2,1)S(1)}, bf16[2,128,128]{2,1,0:T(8,128)(2,1)}, u32[]{:S(2)}) copy-start(bf16[2,128,128]{2,1,0:T(8,128)(2,1)} %constant.5.clone.matrix_ref) | copy-start | bytes 196612
  41.8 9.2 %collective-permute-start = (f32[2,8,128]{2,1,0:T(8,128)S(1)}, f32[2,8,128]{2,1,0:T(8,128)S(1)}, u32[]{:S(2)}, u32[]{:S(2)}) collective-permute-start(f32[2,8,128]{2,1,0:T(8,128)S(1)} %project.1.coef_ref), channel_id=1, source_target_pairs={{0,2},{2,4},{4,6},{6,8},{8,10},{10,12},{12,14},{14,16},{16,18},{18... | collective-permute-start | bytes 24584 | tf_op jit(solution)/shard_map/ppermute | solution.py:22
  41.9 9.0 %collective-permute-start.1 = (f32[2,8,128]{2,1,0:T(8,128)S(1)}, f32[2,8,128]{2,1,0:T(8,128)S(1)}, u32[]{:S(2)}, u32[]{:S(2)}) collective-permute-start(f32[2,8,128]{2,1,0:T(8,128)S(1)} %project.1.coef_ref), channel_id=1, source_target_pairs={{0,30},{2,0},{4,2},{6,4},{8,6},{10,8},{12,10},{14,12},{16,14},{18,... | collective-permute-start | bytes 24584 | tf_op jit(solution)/shard_map/ppermute | solution.py:22
  46.2 6.3 %collective-permute-start.2 = (f32[2,8,128]{2,1,0:T(8,128)S(1)}, f32[2,8,128]{2,1,0:T(8,128)S(1)}, u32[]{:S(2)}, u32[]{:S(2)}) collective-permute-start(f32[2,8,128]{2,1,0:T(8,128)S(1)} %project.1.coef_ref), channel_id=1, source_target_pairs={{0,4},{2,6},{4,8},{6,10},{8,12},{10,14},{12,16},{14,18},{16,20},{1... | collective-permute-start | bytes 24584 | tf_op jit(solution)/shard_map/ppermute | solution.py:22
  46.2 6.3 %collective-permute-start.3 = (f32[2,8,128]{2,1,0:T(8,128)S(1)}, f32[2,8,128]{2,1,0:T(8,128)S(1)}, u32[]{:S(2)}, u32[]{:S(2)}) collective-permute-start(f32[2,8,128]{2,1,0:T(8,128)S(1)} %project.1.coef_ref), channel_id=1, source_target_pairs={{0,28},{2,30},{4,0},{6,2},{8,4},{10,6},{12,8},{14,10},{16,12},{18,... | collective-permute-start | bytes 24584 | tf_op jit(solution)/shard_map/ppermute | solution.py:22
  52.6 26.5 %copy-start.3 = (f32[8,128,128]{2,1,0:T(8,128)S(1)}, f32[8,128,128]{2,1,0:T(8,128)}, u32[]{:S(2)}) copy-start(f32[8,128,128]{2,1,0:T(8,128)} %potential_ref.1) | copy-start | bytes 1572868
  53.8 20.6 %all-to-all-start.3 = ((f32[16,1,64,128]{3,2,1,0:T(8,128)}), f32[16,1,64,128]{3,2,1,0:T(8,128)S(1)}, u32[]{:S(2)}, u32[]{:S(2)}) async-start(f32[16,1,64,128]{3,2,1,0:T(8,128)} %along_x.3), calls=%async_computation.3 | async-start | bytes 1048576 | tf_op jit(solution)/shard_map/all_to_all | solution.py:359
  74.3 18.6 %all-to-all-start.1 = ((f32[16,1,64,128]{3,2,1,0:T(8,128)}), f32[16,1,64,128]{3,2,1,0:T(8,128)S(1)}, u32[]{:S(2)}, u32[]{:S(2)}) async-start(f32[16,1,64,128]{3,2,1,0:T(8,128)} %along_x.2), calls=%async_computation.1 | async-start | bytes 1048576 | tf_op jit(solution)/shard_map/all_to_all | solution.py:359
  80.2 10.2 %collective-permute-start.4 = (f32[8,64,128]{2,1,0:T(8,128)S(1)}, f32[8,64,128]{2,1,0:T(8,128)S(1)}, u32[]{:S(2)}, u32[]{:S(2)}) collective-permute-start(f32[8,64,128]{2,1,0:T(8,128)S(1)} %get-tuple-element.7), channel_id=1, source_target_pairs={{0,1},{1,0},{2,3},{3,2},{4,5},{5,4},{6,7},{7,6},{8,9},{9,8},{10,11... | collective-permute-start | bytes 786440 | tf_op jit(solution)/shard_map/ppermute | solution.py:22

commit v6 on v4

--- a/solution.py
+++ b/solution.py
@@ -1,3 +1,4 @@
+import functools
 import math
 
 import jax
@@ -50,17 +51,17 @@
     return dot(left[0], right[0]) + (dot(left[0], right[1]) + dot(left[1], right[0]))
 
 
-def pack_kernel(wave_ref, send_ref):
-    _, orbitals, planes, extent, _ = wave_ref.shape
+def pack_kernel(planes, wave_ref, send_ref):
+    _, orbitals, _, extent, _ = wave_ref.shape
     count = send_ref.shape[0]
     width = extent // count
-    for p in range(planes):
-        for c in range(2):
-            for o in range(orbitals):
-                for d in range(count):
-                    send_ref[d, c * orbitals + o, pl.ds(p, width, stride=planes), :] = wave_ref[
-                        c, o, p, d * width : (d + 1) * width, :
-                    ]
+    p = pl.program_id(0)
+    for c in range(2):
+        for o in range(orbitals):
+            for d in range(count):
+                send_ref[d, c * orbitals + o, pl.ds(p, width, stride=planes), :] = wave_ref[
+                    c, o, 0, d * width : (d + 1) * width, :
+                ]
 
 
 def along_x_kernel(held_ref, matrix_ref, coef_ref, out_ref, lined):
@@ -297,10 +298,11 @@
     shares = lax.axis_size("orb")
     density_shape = shape((planes, extent // shares, extent))
     send = pl.pallas_call(
-        pack_kernel,
+        functools.partial(pack_kernel, planes),
         out_shape=shape((count, rows, width * planes, extent)),
-        in_specs=[VMEM],
-        out_specs=VMEM,
+        grid=(planes,),
+        in_specs=[pl.BlockSpec((2, orbitals, 1, extent, extent), lambda p: (0, 0, p, 0, 0))],
+        out_specs=pl.BlockSpec((count, rows, width * planes, extent), lambda p: (0, 0, 0, 0)),
         compiler_params=params(),
         cost_estimate=cost(wave.size, 2 * size),
         name="pack",

time: 68.3 us -> 68.3 us (level)
  no operation moved by 1% of the time
where the time goes in v6:
time: 68.3 us
  Pallas kernels  20.4 us (30%)
  starting transfers between devices  18.8 us (28%)
  waiting for transfers between devices  17.7 us (26%)
  local copies, waits for them, and re-layouts  9.33 us (14%)
  between operations  1.42 us (2%)
  other arithmetic  0.74 us (1%)
    all_to_all x1, waiting for transfers between devices, per_device(): back = lax.all_to_all(along, 'grid', 0, 0, tiled=True)  11.2 us
    pallas_call x1, Pallas kernels, per_device(): pl.pallas_call(spread_kernel, out_shape=shape(local.shape), in_specs=[VME...  9.89 us
    ppermute x5, starting transfers between devices, passed_along(): return lax.ppermute(value, axis, pairs)  7.17 us
    ppermute x5, waiting for transfers between devices, passed_along(): return lax.ppermute(value, axis, pairs)  6.41 us
    all_to_all x1, starting transfers between devices, per_device(): held = lax.all_to_all(send, 'grid', 0, 0, tiled=True)  6.16 us
    all_to_all x1, starting transfers between devices, per_device(): back = lax.all_to_all(along, 'grid', 0, 0, tiled=True)  5.44 us
    pallas_call x1, Pallas kernels, per_device(): pl.pallas_call(project_kernel, out_shape=shape((rows, proj_count, atom_co...  5.28 us
    transpose x1, local copies, waits for them, and re-layouts, per_device(): jnp.transpose(table, (0, 1, 3, 2, 4)).reshape(kind_count, box, box, lanes)  3.79 us
  transfers between devices with their start and end apart: 7, of which 3 were waited for; matrix products, arithmetic and copies ran while one was open for 13% of the time, Pallas kernels for 24%

profile of v6, /device:TPU:16, one launch (start us, length us, event | category | flops | bytes accessed | tf_op | source)
XLA Modules:
  0.0 68.3 jit_solution(9416586973339487324)
XLA Ops:
  0.6 0.0 copy-start
  0.6 1.2 %copy-done = f32[2,1,8,128,128]{4,3,2,1,0:T(8,128)S(1)} copy-done((f32[2,1,8,128,128]{4,3,2,1,0:T(8,128)S(1)}, f32[2,1,8,128,128]{4,3,2,1,0:T(8,128)}, u32[]{:S(2)}) %copy-start) | copy-done | bytes 1048600
  1.9 0.0 copy-start.7
  1.9 1.4 %pack.1 = f32[16,2,64,128]{3,2,1,0:T(8,128)} custom-call(f32[2,1,8,128,128]{4,3,2,1,0:T(8,128)S(1)} %copy-done), custom_call_target="tpu_custom_call" | custom-call | flops 262144 | bytes 2097152 | tf_op jit(solution)/shard_map/pack/pallas_call | solution.py:300
  3.2 6.2 %all-to-all-start = ((f32[16,2,64,128]{3,2,1,0:T(8,128)}), f32[16,2,64,128]{3,2,1,0:T(8,128)S(1)}, u32[]{:S(2)}, u32[]{:S(2)}) async-start(f32[16,2,64,128]{3,2,1,0:T(8,128)} %pack.1), calls=%async_computation | async-start | bytes 2097152 | tf_op jit(solution)/shard_map/all_to_all | solution.py:310
  9.4 0.0 copy-done.7
  9.4 2.0 %reshape.16 = f32[2,16,8,16,16]{4,3,2,1,0:T(8,128)} reshape(f32[2,16,8,256]{3,2,1,0:T(8,128)S(1)} %copy-done.7) | data formatting | bytes 524288 | tf_op jit(solution)/shard_map/reshape | solution.py:311
  11.4 3.8 %copy.10 = f32[2,16,16,8,16]{4,3,2,1,0:T(8,128)} copy(f32[2,16,16,8,16]{4,2,3,1,0:T(8,128)} %bitcast.10) | data formatting | bytes 524288 | tf_op jit(solution)/shard_map/transpose | solution.py:312
  15.2 0.0 copy-start.1
  15.2 0.0 copy-start.4
  15.2 0.0 copy-start.5
  15.2 0.0 copy-start.6
  15.2 0.0 copy-start.3
  15.2 2.3 %reshape.17 = f32[2,16,16,128]{3,2,1,0:T(8,128)S(1)} reshape(f32[2,16,16,8,16]{4,3,2,1,0:T(8,128)} %copy.10) | data formatting | bytes 524288 | tf_op jit(solution)/shard_map/reshape | solution.py:312
  17.5 0.0 copy-done.1
  17.5 0.0 copy-done.4
  17.5 0.0 copy-done.5
  17.5 0.0 copy-done.6
  17.5 5.3 %project.1 = f32[2,8,128]{2,1,0:T(8,128)S(1)} custom-call(f32[2,1,8,128,128]{4,3,2,1,0:T(8,128)S(1)} %copy-done.1, f32[34,16,128]{2,1,0:T(8,128)S(1)} %bitcast.7, f32[2,8,8]{2,1,0:T(8,128)S(1)} %copy-done.4, s32[1,128]{1,0:T(1,128)S(1)} %bitcast.9, s32[3,128]{1,0:T(4,128)S(1)} %copy-done.5, s32[128]{0:T(128)S(1)} %copy-done.6), custom_call_target="tpu_custom_call" | custom-call | flops 10485760 | bytes 20971520 | tf_op jit(solution)/shard_map/project/pallas_call | solution.py:315
  22.8 0.0 collective-permute-start
  22.8 2.7 %collective-permute-start.1 = (f32[2,8,128]{2,1,0:T(8,128)S(1)}, f32[2,8,128]{2,1,0:T(8,128)S(1)}, u32[]{:S(2)}, u32[]{:S(2)}) collective-permute-start(f32[2,8,128]{2,1,0:T(8,128)S(1)} %project.1), channel_id=1, source_target_pairs={{0,30},{2,0},{4,2},{6,4},{8,6},{10,8},{12,10},{14,12},{16,14},{18,... | collective-permute-start | bytes 24584 | tf_op jit(solution)/shard_map/ppermute | solution.py:22
  25.5 0.3 collective-permute-start.2
  25.8 2.6 %collective-permute-start.3 = (f32[2,8,128]{2,1,0:T(8,128)S(1)}, f32[2,8,128]{2,1,0:T(8,128)S(1)}, u32[]{:S(2)}, u32[]{:S(2)}) collective-permute-start(f32[2,8,128]{2,1,0:T(8,128)S(1)} %project.1), channel_id=1, source_target_pairs={{0,28},{2,30},{4,0},{6,2},{8,4},{10,6},{12,8},{14,10},{16,12},{18,... | collective-permute-start | bytes 24584 | tf_op jit(solution)/shard_map/ppermute | solution.py:22
  28.4 5.8 %collective-permute-done = f32[2,8,128]{2,1,0:T(8,128)S(1)} collective-permute-done((f32[2,8,128]{2,1,0:T(8,128)S(1)}, f32[2,8,128]{2,1,0:T(8,128)S(1)}, u32[]{:S(2)}, u32[]{:S(2)}) %collective-permute-start) | collective-permute-done | bytes 8224 | tf_op jit(solution)/shard_map/ppermute | solution.py:22
  34.3 0.0 collective-permute-done.1
  34.3 0.6 collective-permute-done.2
  34.8 0.0 collective-permute-done.3
  34.8 0.0 copy-start.2
  34.9 0.0 all-to-all-done.held_ref
  34.9 0.0 copy-done.3
  34.9 1.5 %along_x.1 = f32[16,2,64,128]{3,2,1,0:T(8,128)} custom-call(f32[16,2,64,128]{3,2,1,0:T(8,128)S(1)} %all-to-all-done.held_ref, bf16[2,128,128]{2,1,0:T(8,128)(2,1)S(1)} %copy-done.3, f32[2,8,128]{2,1,0:T(8,128)S(1)} %add_add_fusion.coef_ref), custom_call_target="tpu_custom_call" | custom-call | flops 201326592 | bytes 2097152 | tf_op jit(solution)/shard_map/along_x/pallas_call | solution.py:345
  36.4 5.4 %all-to-all-start.1 = ((f32[16,2,64,128]{3,2,1,0:T(8,128)}), f32[16,2,64,128]{3,2,1,0:T(8,128)S(1)}, u32[]{:S(2)}, u32[]{:S(2)}) async-start(f32[16,2,64,128]{3,2,1,0:T(8,128)} %along_x.1), calls=%async_computation.1 | async-start | bytes 2097152 | tf_op jit(solution)/shard_map/all_to_all | solution.py:355
  42.5 0.0 copy-done.2
  42.5 1.0 %local.1 = (f32[16,144,128]{2,1,0:T(8,128)S(1)}, f32[8,64,128]{2,1,0:T(8,128)S(1)}, f32[8,64,128]{2,1,0:T(8,128)S(1)}) custom-call(f32[2,1,8,128,128]{4,3,2,1,0:T(8,128)S(1)} %copy-done.1, f32[8,128,128]{2,1,0:T(8,128)S(1)} %copy-done.2, bf16[2,128,128]{2,1,0:T(8,128)(2,1)S(1)} %copy-done.3, f32[1]{0:T(128)S(6)} %copy.11.occ_ref), custom_call_target="tpu_custom_call" | custom-call | flops 402653184 | bytes 3145728 | tf_op jit(solution)/shard_map/local/pallas_call | solution.py:333
  43.6 1.6 %collective-permute-start.4 = (f32[8,64,128]{2,1,0:T(8,128)S(1)}, f32[8,64,128]{2,1,0:T(8,128)S(1)}, u32[]{:S(2)}, u32[]{:S(2)}) collective-permute-start(f32[8,64,128]{2,1,0:T(8,128)S(1)} %get-tuple-element.7), channel_id=1, source_target_pairs={{0,1},{1,0},{2,3},{3,2},{4,5},{5,4},{6,7},{7,6},{8,9},{9,8},{10,11... | collective-permute-start | bytes 786440 | tf_op jit(solution)/shard_map/ppermute | solution.py:22
  45.2 9.9 %spread.1.local_ref = f32[16,144,128]{2,1,0:T(8,128)S(1)} custom-call(f32[16,144,128]{2,1,0:T(8,128)S(1)} %get-tuple-element.5.local_ref, f32[34,16,128]{2,1,0:T(8,128)S(1)} %bitcast.8, f32[2,8,128]{2,1,0:T(8,128)S(1)} %add_add_fusion.coef_ref, s32[3,128]{1,0:T(4,128)S(1)} %copy-done.5, s32[128]{0:T(128)S(1)} %copy-done.6), custom_call_target="tpu_custom_call" | custom-call | flops 10485760 | bytes 20971520 | tf_op jit(solution)/shard_map/spread/pallas_call | solution.py:356
  55.0 0.0 collective-permute-done.4
  55.1 0.7 %add.21 = f32[8,64,128]{2,1,0:T(8,128)} add(f32[8,64,128]{2,1,0:T(8,128)S(1)} %get-tuple-element.6, f32[8,64,128]{2,1,0:T(8,128)S(1)} %collective-permute-done.4) | non-fusion elementwise | flops 65536 | bytes 786432 | tf_op jit(solution)/shard_map/add | solution.py:344
  55.8 11.2 %all-to-all-done.1.along_ref = f32[16,2,64,128]{3,2,1,0:T(8,128)S(1)} async-done(((f32[16,2,64,128]{3,2,1,0:T(8,128)}), f32[16,2,64,128]{3,2,1,0:T(8,128)S(1)}, u32[]{:S(2)}, u32[]{:S(2)}) %all-to-all-start.1) | async-done | bytes 1048608 | tf_op jit(solution)/shard_map/all_to_all | solution.py:355
  67.0 1.2 %finish.1 = f32[2,1,8,128,128]{4,3,2,1,0:T(8,128)} custom-call(f32[16,144,128]{2,1,0:T(8,128)S(1)} %spread.1.local_ref, f32[16,2,64,128]{3,2,1,0:T(8,128)S(1)} %all-to-all-done.1.along_ref), custom_call_target="tpu_custom_call" | custom-call | flops 1048576 | bytes 3145728 | tf_op jit(solution)/shard_map/finish/pallas_call | solution.py:369
  (2 shorter events, 0.0 us)
Async XLA Ops:
  0.6 1.2 %copy-start = (f32[2,1,8,128,128]{4,3,2,1,0:T(8,128)S(1)}, f32[2,1,8,128,128]{4,3,2,1,0:T(8,128)}, u32[]{:S(2)}) copy-start(f32[2,1,8,128,128]{4,3,2,1,0:T(8,128)} %wave_ref.5) | copy-start | bytes 3145732
  1.9 7.5 %copy-start.7 = (f32[2,16,8,256]{3,2,1,0:T(8,128)S(1)}, f32[2,16,8,256]{3,2,1,0:T(8,128)}, u32[]{:S(2)}) copy-start(f32[2,16,8,256]{3,2,1,0:T(8,128)} %param.13) | copy-start | bytes 786436
  3.2 31.6 %all-to-all-start = ((f32[16,2,64,128]{3,2,1,0:T(8,128)}), f32[16,2,64,128]{3,2,1,0:T(8,128)S(1)}, u32[]{:S(2)}, u32[]{:S(2)}) async-start(f32[16,2,64,128]{3,2,1,0:T(8,128)} %pack.1), calls=%async_computation | async-start | bytes 2097152 | tf_op jit(solution)/shard_map/all_to_all | solution.py:310
  15.2 2.3 %copy-start.1 = (f32[2,1,8,128,128]{4,3,2,1,0:T(8,128)S(1)}, f32[2,1,8,128,128]{4,3,2,1,0:T(8,128)}, u32[]{:S(2)}) copy-start(f32[2,1,8,128,128]{4,3,2,1,0:T(8,128)} %wave_ref.5) | copy-start | bytes 3145732
  15.2 2.3 %copy-start.4 = (f32[2,8,8]{2,1,0:T(8,128)S(1)}, f32[2,8,8]{2,1,0:T(8,128)}, u32[]{:S(2)}) copy-start(f32[2,8,8]{2,1,0:T(8,128)} %coupling_ref.1) | copy-start | bytes 1540
  15.2 2.3 %copy-start.5 = (s32[3,128]{1,0:T(4,128)S(1)}, s32[3,128]{1,0:T(4,128)}, u32[]{:S(2)}) copy-start(s32[3,128]{1,0:T(4,128)} %centres_ref.3) | copy-start | bytes 4612
  15.2 2.3 %copy-start.6 = (s32[128]{0:T(128)S(1)}, s32[128]{0:T(128)}, u32[]{:S(2)}) copy-start(s32[128]{0:T(128)} %species_ref.3) | copy-start | bytes 1540
  15.2 19.7 %copy-start.3 = (bf16[2,128,128]{2,1,0:T(8,128)(2,1)S(1)}, bf16[2,128,128]{2,1,0:T(8,128)(2,1)}, u32[]{:S(2)}) copy-start(bf16[2,128,128]{2,1,0:T(8,128)(2,1)} %constant.5.clone.matrix_ref) | copy-start | bytes 196612
  22.8 11.4 %collective-permute-start = (f32[2,8,128]{2,1,0:T(8,128)S(1)}, f32[2,8,128]{2,1,0:T(8,128)S(1)}, u32[]{:S(2)}, u32[]{:S(2)}) collective-permute-start(f32[2,8,128]{2,1,0:T(8,128)S(1)} %project.1), channel_id=1, source_target_pairs={{0,2},{2,4},{4,6},{6,8},{8,10},{10,12},{12,14},{14,16},{16,18},{18... | collective-permute-start | bytes 24584 | tf_op jit(solution)/shard_map/ppermute | solution.py:22
  22.8 11.4 %collective-permute-start.1 = (f32[2,8,128]{2,1,0:T(8,128)S(1)}, f32[2,8,128]{2,1,0:T(8,128)S(1)}, u32[]{:S(2)}, u32[]{:S(2)}) collective-permute-start(f32[2,8,128]{2,1,0:T(8,128)S(1)} %project.1), channel_id=1, source_target_pairs={{0,30},{2,0},{4,2},{6,4},{8,6},{10,8},{12,10},{14,12},{16,14},{18,... | collective-permute-start | bytes 24584 | tf_op jit(solution)/shard_map/ppermute | solution.py:22
  25.5 9.3 %collective-permute-start.2 = (f32[2,8,128]{2,1,0:T(8,128)S(1)}, f32[2,8,128]{2,1,0:T(8,128)S(1)}, u32[]{:S(2)}, u32[]{:S(2)}) collective-permute-start(f32[2,8,128]{2,1,0:T(8,128)S(1)} %project.1), channel_id=1, source_target_pairs={{0,4},{2,6},{4,8},{6,10},{8,12},{10,14},{12,16},{14,18},{16,20},{1... | collective-permute-start | bytes 24584 | tf_op jit(solution)/shard_map/ppermute | solution.py:22
  25.8 9.0 %collective-permute-start.3 = (f32[2,8,128]{2,1,0:T(8,128)S(1)}, f32[2,8,128]{2,1,0:T(8,128)S(1)}, u32[]{:S(2)}, u32[]{:S(2)}) collective-permute-start(f32[2,8,128]{2,1,0:T(8,128)S(1)} %project.1), channel_id=1, source_target_pairs={{0,28},{2,30},{4,0},{6,2},{8,4},{10,6},{12,8},{14,10},{16,12},{18,... | collective-permute-start | bytes 24584 | tf_op jit(solution)/shard_map/ppermute | solution.py:22
  34.8 7.7 %copy-start.2 = (f32[8,128,128]{2,1,0:T(8,128)S(1)}, f32[8,128,128]{2,1,0:T(8,128)}, u32[]{:S(2)}) copy-start(f32[8,128,128]{2,1,0:T(8,128)} %potential_ref.1) | copy-start | bytes 1572868
  36.4 30.6 %all-to-all-start.1 = ((f32[16,2,64,128]{3,2,1,0:T(8,128)}), f32[16,2,64,128]{3,2,1,0:T(8,128)S(1)}, u32[]{:S(2)}, u32[]{:S(2)}) async-start(f32[16,2,64,128]{3,2,1,0:T(8,128)} %along_x.1), calls=%async_computation.1 | async-start | bytes 2097152 | tf_op jit(solution)/shard_map/all_to_all | solution.py:355
  43.6 11.5 %collective-permute-start.4 = (f32[8,64,128]{2,1,0:T(8,128)S(1)}, f32[8,64,128]{2,1,0:T(8,128)S(1)}, u32[]{:S(2)}, u32[]{:S(2)}) collective-permute-start(f32[8,64,128]{2,1,0:T(8,128)S(1)} %get-tuple-element.7), channel_id=1, source_target_pairs={{0,1},{1,0},{2,3},{3,2},{4,5},{5,4},{6,7},{7,6},{8,9},{9,8},{10,11... | collective-permute-start | bytes 786440 | tf_op jit(solution)/shard_map/ppermute | solution.py:22
